TPU v7x, 512 devices: a whole 4x8x8 slice. The times are simulated.
512 devices in a mesh: tm: 8 (over x, z_lo), row: 16 (over y, core), col: 4 (over z_hi).
Axes of the slice: x: 4, y: 8, z: 8 (z_hi: 4, z_lo: 2; z = z_hi * 2 + z_lo), core: 2. Of those that a mesh axis runs over, the one named last changes fastest.
Arguments:
- features: bfloat16 [16, 96, 128, 192], P('tm', 'row', 'col'), may hold values from -80 to 80
- cotangent: bfloat16 [16, 96, 128, 192], P('tm', 'row', 'col'), may hold values from -12 to 12
- kernel: bfloat16 [5184, 192], replicated, may hold values from -0.078125 to 0.078125
- gain: float32 [192], replicated, may hold values from 0.1 to 1.9
Outputs:
- feature_grad: bfloat16 [16, 96, 128, 192], P('tm', 'row', 'col')
- weight_grad: float32 [5184, 192], P(('row', 'col'))
- gain_grad: float32 [192], replicated
All inputs are finite; a program needn't handle non-finite values.
Results may differ from a plain program's by a relative error of at most 0.0029.
Values may be sent and summed in bfloat16 or wider, within the bound.
A program may use at most 64 MiB of HBM per device.

v0:
```python
import math

import jax
import jax.numpy as jnp
from jax import lax
from jax.sharding import PartitionSpec as P


def shifted(value, axis, steps):
    count = lax.axis_size(axis)
    first, last = (max(0, -steps), min(count, count - steps))
    return lax.ppermute(value, axis, [(source, source + steps) for source in range(first, last)])


def padded_2(cells, sides, width):
    for axis, dim in sides:
        count = lax.axis_size(axis)
        ends = count - 1
        head = lax.slice_in_dim(cells, 0, width, axis=dim)
        tail = lax.slice_in_dim(cells, cells.shape[dim] - width, cells.shape[dim], axis=dim)
        cells = jnp.concatenate(
            [
                lax.ppermute(tail, axis, [(i, (i + 1) % count) for i in range(ends)]),
                cells,
                lax.ppermute(head, axis, [((i + 1) % count, i) for i in range(ends)]),
            ],
            axis=dim,
        )
    return cells


def tap_stack(padded, offsets, first, frames, height, width):
    slices = [
        padded[
            first + start_t : first + start_t + frames,
            start_r : start_r + height,
            start_c : start_c + width,
        ]
        for start_t, start_r, start_c in offsets
    ]
    stacked = jnp.stack(slices, axis=3)
    return stacked.reshape(frames * height * width, len(offsets), padded.shape[3])


def frame_blocks(frames, height, width):
    step = max(1, -(-512 // (height * width)))
    return [(0, min(step, frames))]


def per_device(features, cotangent, kernel, gain):
    frames, height, width, chan = features.shape
    wide = features.astype(jnp.float32)
    inverse = lax.rsqrt(jnp.mean(wide * wide, axis=-1, keepdims=True) + 1e-06)
    normed = wide * inverse
    pre = normed * gain
    act = jax.nn.silu(pre).astype(jnp.bfloat16)
    earlier = shifted(act, "tm", 1)
    act_ext = jnp.concatenate([earlier, act], axis=0)
    act_pad = padded_2(act_ext, (("row", 1), ("col", 2)), 1)
    later = shifted(cotangent, "tm", -1)
    grad_ext = jnp.concatenate([cotangent, later], axis=0)
    grad_pad = padded_2(grad_ext, (("row", 1), ("col", 2)), 1)
    forward_offsets = [
        (shift_t, shift_r, shift_c)
        for shift_t in range(3)
        for shift_r in range(3)
        for shift_c in range(3)
    ]
    backward_offsets = [
        (2 - shift_t, 2 - shift_r, 2 - shift_c) for shift_t, shift_r, shift_c in forward_offsets
    ]
    blocks = frame_blocks(frames, height, width)
    kernel_taps = kernel.reshape(27, chan, chan)
    dact_parts = []
    for first, count in blocks:
        grad_patches = tap_stack(grad_pad, backward_offsets, first, count, height, width)
        dact_parts.append(
            jnp.einsum("nko,kio->ni", grad_patches, kernel_taps, preferred_element_type=jnp.float32)
        )
    dact = dact_parts[0].reshape(features.shape)
    total_cells = (
        frames * height * width * lax.axis_size("tm") * lax.axis_size("row") * lax.axis_size("col")
    )
    scale = 1.0 / math.sqrt(total_cells)
    sigma = jax.nn.sigmoid(pre)
    dpre = dact * sigma * (1.0 + pre * (1.0 - sigma))
    gain_part = jnp.sum(dpre * normed, axis=(0, 1, 2))
    gain_grad = lax.psum(gain_part, ("tm", "row", "col")) * scale
    dnormed = dpre * gain
    project = jnp.mean(dnormed * normed, axis=-1, keepdims=True)
    feature_grad = (cotangent.astype(jnp.float32) + inverse * (dnormed - normed * project)).astype(
        jnp.bfloat16
    )
    contract = (((0,), (0,)), ((), ()))
    total = jnp.zeros((27 * chan, chan), jnp.float32)
    for first, count in blocks:
        patches = tap_stack(act_pad, forward_offsets, first, count, height, width).reshape(
            count * height * width, 27 * chan
        )
        grad_rows = cotangent.reshape(count * height * width, chan)
        total = lax.dot_general(patches, grad_rows, contract, preferred_element_type=jnp.float32)
    partial_value = lax.psum_scatter(total, ("row", "col"), scatter_dimension=0, tiled=True)
    weight_shard = lax.psum(partial_value, "tm")
    weight_grad = weight_shard * scale
    return (feature_grad, weight_grad, gain_grad)


def solution(mesh):
    return jax.shard_map(
        per_device,
        mesh=mesh,
        in_specs=(P("tm", "row", "col", None), P("tm", "row", "col", None), P(), P()),
        out_specs=(P("tm", "row", "col", None), P(("row", "col"), None), P()),
        check_vma=False,
    )
```

profile of v0, /device:TPU:1, one launch (start us, length us, event | category | flops | bytes accessed | tf_op | source)
XLA Modules:
  0.0 439.6 jit_solution(17592160914231398444)
XLA Ops:
  0.6 1.3 collective-permute-start
  2.9 5.8 %collective-permute-done = bf16[2,6,32,192]{3,2,1,0:T(8,128)(2,1)S(1)} collective-permute-done((bf16[2,6,32,192]{3,2,1,0:T(8,128)(2,1)}, bf16[2,6,32,192]{3,2,1,0:T(8,128)(2,1)S(1)}, u32[]{:S(2)}, u32[]{:S(2)}) %collective-permute-start) | collective-permute-done | bytes 147488 | tf_op jit(solution)/shard_map/ppermute | solution.py:12
  8.8 8.5 %collective-permute-start.2 = (bf16[4,1,32,192]{3,2,1,0:T(8,128)(2,1)S(1)}, bf16[4,1,32,192]{3,2,1,0:T(8,128)(2,1)S(1)}, u32[]{:S(2)}, u32[]{:S(2)}) collective-permute-start(bf16[4,1,32,192]{3,2,1,0:T(8,128)(2,1)S(1)} %get-tuple-element.18), channel_id=1, source_target_pairs={{4,0},{8,4},{12,8},{16,12},{20,16},{24,20},{28,24},{32,28},{36,32}... | collective-permute-start | bytes 147464 | tf_op jit(solution)/shard_map/ppermute | solution.py:25
  17.2 1.9 collective-permute-start.1
  19.2 1.1 fusion.21
  20.5 3.2 collective-permute-start.4
  23.8 1.3 collective-permute-start.3
  25.1 3.9 copy.85
  29.0 2.5 collective-permute-done.3
  33.9 1.7 fusion.20
  36.6 4.0 collective-permute-start.5
  40.6 4.0 collective-permute-done.5
  44.7 3.0 collective-permute-start.7
  47.7 4.0 collective-permute-start.6
  51.6 1.3 dynamic-slice.4
  53.0 1.3 collective-permute-start.9
  54.3 6.4 %collective-permute-start.8 = (bf16[4,8,1,192]{3,2,1,0:T(2,128)(2,1)S(1)}, bf16[4,8,1,192]{3,2,1,0:T(2,128)(2,1)S(1)}, u32[]{:S(2)}, u32[]{:S(2)}) collective-permute-start(bf16[4,8,1,192]{3,2,1,0:T(2,128)(2,1)S(1)} %get-tuple-element.8), channel_id=1, source_target_pairs={{0,1},{1,2},{2,3},{4,5},{5,6},{6,7},{8,9},{9,10},{10,11},{12,13},{... | collective-permute-start | bytes 36872 | tf_op jit(solution)/shard_map/ppermute | solution.py:23
  62.9 6.4 %copy.86 = bf16[2,6,32,27,192]{4,3,2,1,0:T(8,128)(2,1)} copy(bf16[2,6,32,27,192]{4,2,1,0,3:T(8,128)(2,1)S(1)} %fusion.34) | data formatting | bytes 7962624 | tf_op jit(solution)/shard_map/stack | solution.py:41
  69.3 10.1 %reshape_reshape.3 = bf16[384,5184]{1,0:T(8,128)(2,1)} reshape(bf16[2,6,32,27,192]{4,3,2,1,0:T(8,128)(2,1)} %copy.86) | data formatting | bytes 7962624 | tf_op jit(solution)/shard_map/reshape;reshape | solution.py:97
  79.4 6.1 %fusion.84 = f32[5184,192]{1,0:T(8,128)} fusion(bf16[384,5184]{1,0:T(8,128)(2,1)} %reshape_reshape.3, bf16[384,192]{1,0:T(8,128)(2,1)S(1)} %bitcast.278), kind=kOutput, calls=%fused_computation.166 | convolution fusion | flops 764411904 | bytes 8110080 | tf_op jit(solution)/shard_map/dot_general | solution.py:101
  85.5 186.2 %fusion = f32[88,192]{1,0:T(8,128)S(1)} fusion(f32[5184,192]{1,0:T(8,128)} %fusion.84), kind=kCustom, calls=%all-reduce-scatter | all-reduce-scatter fusion | flops 1081345 | bytes 4050944
  271.7 1.6 collective-permute-start.15
  274.0 115.2 %psum.15 = f32[192]{0:T(256)S(1)} all-reduce(f32[192]{0:T(256)S(1)} %get-tuple-element.3), channel_id=1, replica_groups=mesh['tm'=8,'row'=16,'col'=4] {'tm','row','col'}, use_global_device_ids=true, to_apply=%region_5.6 | all-reduce | flops 192 | bytes 1536 | tf_op jit(solution)/shard_map/psum | solution.py:88
  389.2 2.6 collective-permute-start.14
  391.8 1.9 collective-permute-start.13
  393.8 6.7 %collective-permute-start.12 = (f32[88,192]{1,0:T(8,128)S(1)}, f32[88,192]{1,0:T(8,128)S(1)}, u32[]{:S(2)}, u32[]{:S(2)}) collective-permute-start(f32[88,192]{1,0:T(8,128)S(1)} %fusion), channel_id=1, source_target_pairs={{0,3},{1,4},{2,5},{3,6},{4,7},{5,8},{6,9},{7,10},{8,11},{9,12},{10... | collective-permute-start | bytes 202760
  400.4 4.1 collective-permute-start.11
  404.5 1.9 collective-permute-start.10
  407.0 3.3 collective-permute-done.11
  410.4 2.2 collective-permute-done.10
  412.6 1.1 concatenate.92
  413.7 25.2 %psum.14 = f32[81,192]{1,0:T(8,128)S(1)} all-reduce(f32[81,192]{1,0:T(8,128)S(1)} %constant_dynamic-slice_fusion), channel_id=1, replica_groups=mesh['tm'=8,'row'=16,'col'=4] {'tm'}, use_global_device_ids=true, to_apply=%region_3.4 | all-reduce | flops 15552 | bytes 124416 | tf_op jit(solution)/shard_map/psum | solution.py:103
  (89 shorter events, 7.9 us)
Async XLA Ops:
  0.6 8.1 %collective-permute-start = (bf16[2,6,32,192]{3,2,1,0:T(8,128)(2,1)}, bf16[2,6,32,192]{3,2,1,0:T(8,128)(2,1)S(1)}, u32[]{:S(2)}, u32[]{:S(2)}) collective-permute-start(bf16[2,6,32,192]{3,2,1,0:T(8,128)(2,1)} %param.5), channel_id=1, source_target_pairs={{64,0},{128,64},{192,128},{256,192},{320,256},{384,320},{448,384},... | collective-permute-start | bytes 442376 | tf_op jit(solution)/shard_map/ppermute | solution.py:12
  8.7 22.7 %copy-start.1 = (bf16[2,6,32,192]{3,2,1,0:T(8,128)(2,1)}, bf16[2,6,32,192]{3,2,1,0:T(8,128)(2,1)S(1)}, u32[]{:S(2)}) copy-start(bf16[2,6,32,192]{3,2,1,0:T(8,128)(2,1)S(1)} %collective-permute-done) | copy-start | bytes 442372
  8.8 11.5 %collective-permute-start.2 = (bf16[4,1,32,192]{3,2,1,0:T(8,128)(2,1)S(1)}, bf16[4,1,32,192]{3,2,1,0:T(8,128)(2,1)S(1)}, u32[]{:S(2)}, u32[]{:S(2)}) collective-permute-start(bf16[4,1,32,192]{3,2,1,0:T(8,128)(2,1)S(1)} %get-tuple-element.18), channel_id=1, source_target_pairs={{4,0},{8,4},{12,8},{16,12},{20,16},{24,20},{28,24},{32,28},{36,32}... | collective-permute-start | bytes 147464 | tf_op jit(solution)/shard_map/ppermute | solution.py:25
  17.2 3.2 collective-permute-start.1
  20.5 8.4 %collective-permute-start.4 = (bf16[4,8,1,192]{3,2,1,0:T(2,128)(2,1)S(1)}, bf16[4,8,1,192]{3,2,1,0:T(2,128)(2,1)S(1)}, u32[]{:S(2)}, u32[]{:S(2)}) collective-permute-start(bf16[4,8,1,192]{3,2,1,0:T(2,128)(2,1)S(1)} %get-tuple-element.11), channel_id=1, source_target_pairs={{0,1},{1,2},{2,3},{4,5},{5,6},{6,7},{8,9},{9,10},{10,11},{12,13},{... | collective-permute-start | bytes 36872 | tf_op jit(solution)/shard_map/ppermute | solution.py:23
  23.8 7.7 %collective-permute-start.3 = (bf16[4,8,1,192]{3,2,1,0:T(2,128)(2,1)S(1)}, bf16[4,8,1,192]{3,2,1,0:T(2,128)(2,1)S(1)}, u32[]{:S(2)}, u32[]{:S(2)}) collective-permute-start(bf16[4,8,1,192]{3,2,1,0:T(2,128)(2,1)S(1)} %get-tuple-element.12), channel_id=1, source_target_pairs={{1,0},{2,1},{3,2},{5,4},{6,5},{7,6},{9,8},{10,9},{11,10},{13,12},{... | collective-permute-start | bytes 36872 | tf_op jit(solution)/shard_map/ppermute | solution.py:25
  31.8 1.9 copy-start
  31.9 2.0 copy-start.2
  31.9 2.0 copy-start.3
  36.6 8.0 %collective-permute-start.5 = (bf16[2,6,32,192]{3,2,1,0:T(8,128)(2,1)S(1)}, bf16[2,6,32,192]{3,2,1,0:T(8,128)(2,1)S(1)}, u32[]{:S(2)}, u32[]{:S(2)}) collective-permute-start(bf16[2,6,32,192]{3,2,1,0:T(8,128)(2,1)S(1)} %get-tuple-element.19), channel_id=1, source_target_pairs={{0,64},{64,128},{128,192},{192,256},{256,320},{320,384},{384,448},... | collective-permute-start | bytes 442376 | tf_op jit(solution)/shard_map/ppermute | solution.py:12
  44.7 8.2 %collective-permute-start.7 = (bf16[4,1,32,192]{3,2,1,0:T(8,128)(2,1)S(1)}, bf16[4,1,32,192]{3,2,1,0:T(8,128)(2,1)S(1)}, u32[]{:S(2)}, u32[]{:S(2)}) collective-permute-start(bf16[4,1,32,192]{3,2,1,0:T(8,128)(2,1)S(1)} %get-tuple-element.16), channel_id=1, source_target_pairs={{4,0},{8,4},{12,8},{16,12},{20,16},{24,20},{28,24},{32,28},{36,32}... | collective-permute-start | bytes 147464 | tf_op jit(solution)/shard_map/ppermute | solution.py:25
  47.7 5.3 %collective-permute-start.6 = (bf16[4,1,32,192]{3,2,1,0:T(8,128)(2,1)S(1)}, bf16[4,1,32,192]{3,2,1,0:T(8,128)(2,1)S(1)}, u32[]{:S(2)}, u32[]{:S(2)}) collective-permute-start(bf16[4,1,32,192]{3,2,1,0:T(8,128)(2,1)S(1)} %get-tuple-element.15), channel_id=1, source_target_pairs={{0,4},{4,8},{8,12},{12,16},{16,20},{20,24},{24,28},{28,32},{32,36}... | collective-permute-start | bytes 147464 | tf_op jit(solution)/shard_map/ppermute | solution.py:23
  53.0 7.9 %collective-permute-start.9 = (bf16[4,8,1,192]{3,2,1,0:T(2,128)(2,1)S(1)}, bf16[4,8,1,192]{3,2,1,0:T(2,128)(2,1)S(1)}, u32[]{:S(2)}, u32[]{:S(2)}) collective-permute-start(bf16[4,8,1,192]{3,2,1,0:T(2,128)(2,1)S(1)} %get-tuple-element.7), channel_id=1, source_target_pairs={{1,0},{2,1},{3,2},{5,4},{6,5},{7,6},{9,8},{10,9},{11,10},{13,12},{... | collective-permute-start | bytes 36872 | tf_op jit(solution)/shard_map/ppermute | solution.py:25
  54.3 7.2 %collective-permute-start.8 = (bf16[4,8,1,192]{3,2,1,0:T(2,128)(2,1)S(1)}, bf16[4,8,1,192]{3,2,1,0:T(2,128)(2,1)S(1)}, u32[]{:S(2)}, u32[]{:S(2)}) collective-permute-start(bf16[4,8,1,192]{3,2,1,0:T(2,128)(2,1)S(1)} %get-tuple-element.8), channel_id=1, source_target_pairs={{0,1},{1,2},{2,3},{4,5},{5,6},{6,7},{8,9},{9,10},{10,11},{12,13},{... | collective-permute-start | bytes 36872 | tf_op jit(solution)/shard_map/ppermute | solution.py:23
  271.7 132.8 %collective-permute-start.15 = (f32[1,192]{1,0:T(1,128)S(1)}, f32[1,192]{1,0:T(1,128)S(1)}, u32[]{:S(2)}, u32[]{:S(2)}) collective-permute-start(f32[1,192]{1,0:T(1,128)S(1)} %slice.333), channel_id=1, source_target_pairs={{0,6},{1,7},{2,8},{3,9},{4,10},{5,11},{6,12},{7,13},{8,14},{9,15},... | collective-permute-start | bytes 2312
  389.2 17.8 %collective-permute-start.14 = (f32[88,192]{1,0:T(8,128)S(1)}, f32[88,192]{1,0:T(8,128)S(1)}, u32[]{:S(2)}, u32[]{:S(2)}) collective-permute-start(f32[88,192]{1,0:T(8,128)S(1)} %fusion), channel_id=1, source_target_pairs={{0,5},{1,6},{2,7},{3,8},{4,9},{5,10},{6,11},{7,12},{8,13},{9,14},{... | collective-permute-start | bytes 202760
  391.8 15.2 %collective-permute-start.13 = (f32[88,192]{1,0:T(8,128)S(1)}, f32[88,192]{1,0:T(8,128)S(1)}, u32[]{:S(2)}, u32[]{:S(2)}) collective-permute-start(f32[88,192]{1,0:T(8,128)S(1)} %fusion), channel_id=1, source_target_pairs={{0,4},{1,5},{2,6},{3,7},{4,8},{5,9},{6,10},{7,11},{8,12},{9,13},{1... | collective-permute-start | bytes 202760
  393.8 13.3 %collective-permute-start.12 = (f32[88,192]{1,0:T(8,128)S(1)}, f32[88,192]{1,0:T(8,128)S(1)}, u32[]{:S(2)}, u32[]{:S(2)}) collective-permute-start(f32[88,192]{1,0:T(8,128)S(1)} %fusion), channel_id=1, source_target_pairs={{0,3},{1,4},{2,5},{3,6},{4,7},{5,8},{6,9},{7,10},{8,11},{9,12},{10... | collective-permute-start | bytes 202760
  400.4 9.9 %collective-permute-start.11 = (f32[88,192]{1,0:T(8,128)S(1)}, f32[88,192]{1,0:T(8,128)S(1)}, u32[]{:S(2)}, u32[]{:S(2)}) collective-permute-start(f32[88,192]{1,0:T(8,128)S(1)} %fusion), channel_id=1, source_target_pairs={{0,2},{1,3},{2,4},{3,5},{4,6},{5,7},{6,8},{7,9},{8,10},{9,11},{10,... | collective-permute-start | bytes 202760
  404.5 8.0 %collective-permute-start.10 = (f32[88,192]{1,0:T(8,128)S(1)}, f32[88,192]{1,0:T(8,128)S(1)}, u32[]{:S(2)}, u32[]{:S(2)}) collective-permute-start(f32[88,192]{1,0:T(8,128)S(1)} %fusion), channel_id=1, source_target_pairs={{0,1},{1,2},{2,3},{3,4},{4,5},{5,6},{6,7},{7,8},{8,9},{9,10},{10,1... | collective-permute-start | bytes 202760
where the time goes:
time: 448 us; the launch traced here: 440 us
  blocking collectives  327 us (73%)
  starting transfers between devices  53.6 us (12%)
  local copies, waits for them, and re-layouts  26.3 us (6%)
  waiting for transfers between devices  18.8 us (4%)
  matrix products  7.78 us (2%)
    unnamed x1, blocking collectives  186 us
    psum x1, blocking collectives, per_device(): gain_grad = lax.psum(gain_part, ('tm', 'row', 'col')) * scale  115 us
    psum x1, blocking collectives, per_device(): weight_shard = lax.psum(partial_value, 'tm')  25.2 us
    unnamed x6, starting transfers between devices  18.9 us
    ppermute x4, starting transfers between devices, padded_2(): lax.ppermute(tail, axis, [(i, (i + 1) % count) for i in range(ends)])  15.5 us
    ppermute x4, starting transfers between devices, padded_2(): lax.ppermute(head, axis, [((i + 1) % count, i) for i in range(ends)])  14 us
    another operation x1, local copies, waits for them, and re-layouts, per_device(): tap_stack(act_pad, forward_offsets, first, count, height, width)  10.1 us
    ppermute x2, waiting for transfers between devices, shifted(): lax.ppermute(value, axis, [(source, source + steps) for source in range(f...  9.88 us
  transfers between devices with their start and end apart: 16, of which 7 were waited for; matrix products, arithmetic and copies ran while one was open for 2% of the time, Pallas kernels for 0%

commit v1 on v0

v1 whole, which is shorter than its diff:
```python
import math

import jax
import jax.numpy as jnp
from jax import lax
from jax.experimental import pallas as pl
from jax.experimental.pallas import tpu as pltpu
from jax.sharding import PartitionSpec as P

MESH = pl.DeviceIdType.MESH
F32 = jnp.float32
BF16 = jnp.bfloat16
C = 192
ROWS, COLS = 6, 32
CELLS = 2 * ROWS * COLS
PIECES = 4
HALF_TAPS = 14
WIN = 144

HALO = [(-1, 0, 0)]
HALO += [(dt, dr, 0) for dt in (0, -1) for dr in (-1, 1)]
HALO += [(dt, dr, dc) for dt in (0, -1) for dc in (-1, 1) for dr in (-1, 0, 1)]


def body(
    feat, cot, w_hbm, gain, fg_out, wg_out, gg_out,
    w_v, big, cols, act_t, packs, rows16, act32, dact_v, wgl, xsend, xrecv,
    gpart, grecv, ysend, yrecv, zsend, zrecv, bsend, brecv, fin,
    w_sem, halo_s, halo_r, pair_s, pair_r, x_s, x_r, g_s, g_r, y_s, y_r, z_s, z_r, b_s, b_r,
):
    tm, row, col = lax.axis_index("tm"), lax.axis_index("row"), lax.axis_index("col")
    x, zlo = tm // 2, tm % 2
    y, core = row // 2, row % 2
    z = col * 2 + zlo
    other = 1 - core
    self_y = core == y // 4
    self_b = x == col

    def near(dt, dr, dc):
        return ((tm + dt + 8) % 8, (row + dr + 16) % 16, (col + dc + 4) % 4)

    partner = (tm, 2 * y + other, col)

    def x_dev(step):
        return (((x + step) % 4) * 2 + zlo, row, col)

    def remote(src, dst, send, recv, device):
        return pltpu.make_async_remote_copy(
            src_ref=src, dst_ref=dst, send_sem=send, recv_sem=recv, device_id=device, device_id_type=MESH
        )

    weights = pltpu.make_async_copy(w_hbm, w_v, w_sem)
    weights.start()

    barrier = pltpu.get_barrier_semaphore()

    def greet(device):
        pl.semaphore_signal(barrier, inc=1, device_id=device, device_id_type=MESH)

    for dt, dr, dc in HALO:
        greet(near(-dt, -dr, -dc))
    greet(partner)
    for step in (1, 2, 3):
        greet(x_dev(-step + 4))
    for k in range(8):
        @pl.when(jnp.logical_not(jnp.logical_and(self_y, y == k)))
        def _():
            greet((tm, 2 * k + y // 4, col))

        @pl.when(z != k)
        def _():
            greet((2 * x + k % 2, row, k // 2))

        @pl.when(jnp.logical_not(jnp.logical_and(self_b, z == k)))
        def _():
            greet((2 * col + k % 2, row, k // 2))

    for side, q in ((0, 0), (1, COLS - 1)):
        rows16[side] = jnp.zeros((16, C), F32)
        for f in range(2):
            for r in range(ROWS):
                i = f * ROWS + r
                rows16[side, i : i + 1, :] = cot[f, r].astype(F32)[q : q + 1, :]
        packs[side] = rows16[side].astype(BF16)

    expected = 17 + 1 + 3 + 7 + 16
    pl.semaphore_wait(barrier, expected - self_y.astype(jnp.int32) - self_b.astype(jnp.int32))

    main = big.at[0, 1]
    halo = []
    for m, (dt, dr, dc) in enumerate(HALO):
        df = -dt
        if dc != 0:
            src = packs.at[0 if dc < 0 else 1]
            dst = cols.at[0, 1 if dc < 0 else 0, df, 1 - dr]
        elif dr == -1:
            src, dst = cot.at[:, 0], main.at[2 * df : 2 * df + 2, ROWS + 1]
        elif dr == 1:
            src, dst = cot.at[:, ROWS - 1], main.at[2 * df : 2 * df + 2, 0]
        else:
            src, dst = cot, main.at[2:4, 1 : ROWS + 1]
        halo.append(remote(src, dst, halo_s.at[m], halo_r.at[m], near(dt, dr, dc)))
        halo[-1].start()
    main[0:2, 1 : ROWS + 1] = cot[...]

    def norm():
        wide = feat[...].astype(F32).reshape(CELLS, C)
        inverse = lax.rsqrt(jnp.mean(wide * wide, axis=-1, keepdims=True) + 1e-06)
        normed = wide * inverse
        return inverse, normed, normed * gain[...]

    pre = norm()[2]
    act32[:, C:] = jnp.zeros((CELLS, 256 - C), F32)
    act32[:, :C] = pre * jax.nn.sigmoid(pre)
    act_t[0] = act32[...].T[:C].astype(BF16)
    swap = [remote(act_t.at[0], act_t.at[1], pair_s.at[0], pair_r.at[0], partner)]
    swap[0].start()

    for copy in halo:
        copy.wait_recv()

    @pl.when(row == 0)
    def _():
        main[:, 0] = jnp.zeros((4, COLS, C), BF16)
        cols[0, :, :, 0] = jnp.zeros((2, 2, 16, C), BF16)

    @pl.when(row == 15)
    def _():
        main[:, ROWS + 1] = jnp.zeros((4, COLS, C), BF16)
        cols[0, :, :, 2] = jnp.zeros((2, 2, 16, C), BF16)

    @pl.when(tm == 7)
    def _():
        main[2:4] = jnp.zeros((2, ROWS + 2, COLS, C), BF16)
        cols[0, :, 1] = jnp.zeros((2, 3, 16, C), BF16)

    @pl.when(col == 0)
    def _():
        cols[0, 0] = jnp.zeros((2, 3, 16, C), BF16)

    @pl.when(col == 3)
    def _():
        cols[0, 1] = jnp.zeros((2, 3, 16, C), BF16)

    swap.append(remote(main, big.at[1, 1], pair_s.at[1], pair_r.at[1], partner))
    swap.append(remote(cols.at[0], cols.at[1], pair_s.at[2], pair_r.at[2], partner))
    swap[1].start()
    swap[2].start()

    spot = lax.broadcasted_iota(jnp.int32, (COLS, C), 0)

    def shift(tile):
        for f in range(4):
            edges = [[cols[tile, s, f // 2, k].astype(F32) for k in range(3)] for s in (0, 1)]
            for r in range(ROWS + 2):
                k = 0 if r == 0 else 2 if r == ROWS + 1 else 1
                i = (f % 2) * ROWS + (r - 1) % ROWS
                value = big[tile, 1, f, r].astype(F32)
                after = jnp.where(spot == COLS - 1, edges[1][k][i : i + 1], pltpu.roll(value, COLS - 1, 0))
                before = jnp.where(spot == 0, edges[0][k][i : i + 1], pltpu.roll(value, 1, 0))
                big[tile, 0, f, r] = after.astype(BF16)
                big[tile, 2, f, r] = before.astype(BF16)

    shift(0)
    for copy in swap:
        copy.wait_recv()
    shift(1)

    lane = lax.broadcasted_iota(jnp.int32, (48, 128), 1)

    def pack(j):
        start = 96 + 80 * j + 16 * (j // 16)
        at = (j // 4) * WIN
        xsend[j % 4, at : at + 96] = wgl[start : start + 96, 0:128].astype(BF16)
        low = wgl[start : start + 48, 128:256]
        high = pltpu.roll(wgl[start + 48 : start + 96, 128:256], 64, 1)
        xsend[j % 4, at + 96 : at + WIN] = jnp.where(lane < 64, low, high).astype(BF16)

    span = 8 // PIECES * WIN
    sent = []

    def x_copy(p, step):
        part = slice(p * span, (p + 1) * span)
        return remote(
            xsend.at[(x + step) % 4, part], xrecv.at[step - 1, part],
            x_s.at[p, step - 1], x_r.at[p, step - 1], x_dev(step),
        )

    ready = 0
    for i in range(HALF_TAPS):
        tap = i + 13 * core
        a, b, c = tap // 9, (tap // 3) % 3, tap % 3
        total = jnp.zeros((C, C), F32)
        for tile in (0, 1):
            patch = big[tile, c, pl.ds(2 - a, 2), pl.ds(2 - b, ROWS)].reshape(CELLS, C)
            total += jnp.dot(act_t[tile], patch, preferred_element_type=F32)
        wgl[pl.ds(pl.multiple_of(i * C + 96 * other, 8), C), 0:C] = total
        while ready < 32 and C * (i + 1) >= C + 80 * ready + 16 * (ready // 16):
            pack(ready)
            ready += 1
            if ready % (32 // PIECES) == 0:
                for step in (1, 2, 3):
                    sent.append(x_copy(ready // (32 // PIECES) - 1, step))
                    sent[-1].start()

    weights.wait()
    dact = jnp.zeros((CELLS, C), F32)
    for tap in range(27):
        a, b, c = tap // 9, (tap // 3) % 3, tap % 3
        patch = big[0, c, 2 - a : 4 - a, 2 - b : 2 - b + ROWS].reshape(CELLS, C)
        dact += lax.dot_general(
            patch, w_v[tap * C : (tap + 1) * C], (((1,), (1,)), ((), ())), preferred_element_type=F32
        )
    inverse, normed, pre = norm()
    sigma = jax.nn.sigmoid(pre)
    dpre = dact * sigma * (1.0 + pre * (1.0 - sigma))
    gain_part = jnp.sum(dpre * normed, axis=0, keepdims=True)
    dnormed = dpre * gain[...]
    project = jnp.mean(dnormed * normed, axis=-1, keepdims=True)
    grad = cot[...].astype(F32).reshape(CELLS, C) + inverse * (dnormed - normed * project)
    fg_out[...] = grad.astype(BF16).reshape(2, ROWS, COLS, C)

    act32[0:1, C:] = jnp.zeros((1, 256 - C), F32)
    act32[0:1, :C] = gain_part
    gpart[...] = jnp.zeros((2, 8, 128), F32)
    gpart[0, 0:1] = act32[0:1, 0:128]
    gpart[0, 1:2] = act32[0:1, 128:256]
    pair_gain = remote(gpart.at[0], grecv.at[0], g_s.at[0], g_r.at[0], partner)
    pair_gain.start()
    pair_gain.wait()
    gpart[1] = gpart[0] + grecv[0]
    gain_copies = []
    for step in (1, 2, 3):
        gain_copies.append(remote(gpart.at[1], grecv.at[step], g_s.at[step], g_r.at[step], x_dev(step)))
        gain_copies[-1].start()
    for copy in gain_copies:
        copy.wait()
    gsum = gpart[1] + grecv[1] + grecv[2] + grecv[3]
    upper = gsum.astype(BF16)
    lower = (gsum - upper.astype(F32)).astype(BF16)
    gain_rows = jnp.concatenate([upper.astype(F32), lower.astype(F32)], axis=0).astype(BF16)

    def y_self(k):
        return jnp.logical_and(self_y, y == k)

    def y_copy(k):
        return remote(ysend.at[k], yrecv.at[y], y_s.at[k], y_r.at[y], (tm, 8 * core + k, col))

    for p in range(PIECES):
        for step in (1, 2, 3):
            x_copy(p, step).wait_recv()
        part = slice(p * span, (p + 1) * span)
        value = xsend[x, part].astype(F32)
        for step in (1, 2, 3):
            value += xrecv[step - 1, part].astype(F32)
        value = value.astype(BF16)
        for k in range(p * 8 // PIECES, (p + 1) * 8 // PIECES):
            at = k * WIN - p * span
            ysend[k, 0:WIN] = value[at : at + WIN]
            ysend[k, WIN : WIN + 16] = gain_rows
            mine = row == 8 * core + k

            @pl.when(jnp.logical_not(mine))
            def _():
                y_copy(k).start()

            @pl.when(mine)
            def _():
                yrecv[y] = ysend[k]

    for k in range(8):
        @pl.when(jnp.logical_not(y_self(k)))
        def _():
            remote(ysend.at[0], yrecv.at[k], y_s.at[0], y_r.at[k], (tm, row, col)).wait_recv()

    total = yrecv[0].astype(F32)
    for k in range(1, 8):
        total += yrecv[k].astype(F32)
    zsend[0:WIN] = total[0:WIN]
    zsend[WIN : WIN + 8] = total[WIN : WIN + 8] + total[WIN + 8 : WIN + 16]
    zsend[WIN + 8 :] = jnp.zeros((40, 128), F32)

    def z_copy(k):
        return remote(
            zsend.at[24 * k : 24 * k + 24], zrecv.at[z], z_s.at[k], z_r.at[z],
            (2 * x + k % 2, row, k // 2),
        )

    for k in range(8):
        @pl.when(z != k)
        def _():
            z_copy(k).start()

        @pl.when(z == k)
        def _():
            zrecv[k] = zsend[24 * k : 24 * k + 24]

    for k in range(8):
        @pl.when(z != k)
        def _():
            remote(zsend.at[0:24], zrecv.at[k], z_s.at[0], z_r.at[k], (tm, row, col)).wait_recv()

    total = zrecv[0]
    for k in range(1, 8):
        total += zrecv[k]
    bsend[...] = total

    def b_self(k):
        return jnp.logical_and(self_b, tm == k)

    def b_copy(k):
        return remote(bsend, brecv.at[z], b_s.at[k], b_r.at[z], (k, row, x))

    for k in range(8):
        @pl.when(jnp.logical_not(b_self(k)))
        def _():
            b_copy(k).start()

        @pl.when(b_self(k))
        def _():
            brecv[z] = bsend[...]

    for k in range(8):
        @pl.when(jnp.logical_not(jnp.logical_and(self_b, z == k)))
        def _():
            remote(bsend, brecv.at[k], b_s.at[0], b_r.at[k], (tm, row, col)).wait_recv()

    scale = 1.0 / math.sqrt(16 * 96 * 128)
    total = brecv[...].reshape(192, 128) * scale
    gg_out[...] = jnp.concatenate([total[WIN : WIN + 1], total[WIN + 1 : WIN + 2]], axis=1)
    fin[:, 0:128] = total[0:96]
    fin[0:48, 128:256] = total[96:WIN]
    fin[48:96, 128:256] = pltpu.roll(total[96:WIN], 64, 1)
    shard = row * 4 + col
    wg_out[...] = pltpu.roll(fin[...], (96 - shard % 16) % 96, 0)[0:81, 0:C]

    for copy in halo + swap + sent:
        copy.wait_send()
    for k in range(8):
        @pl.when(row != 8 * core + k)
        def _():
            y_copy(k).wait_send()

        @pl.when(z != k)
        def _():
            z_copy(k).wait_send()

        @pl.when(jnp.logical_not(b_self(k)))
        def _():
            b_copy(k).wait_send()


def per_device(features, cotangent, kernel, gain):
    vmem = pl.BlockSpec(memory_space=pltpu.VMEM)
    dma = pltpu.SemaphoreType.DMA
    fg, wg, gg = pl.pallas_call(
        body,
        out_shape=(
            jax.ShapeDtypeStruct((2, ROWS, COLS, C), BF16),
            jax.ShapeDtypeStruct((81, C), F32),
            jax.ShapeDtypeStruct((1, 256), F32),
        ),
        in_specs=[vmem, vmem, pl.BlockSpec(memory_space=pl.ANY), vmem],
        out_specs=(vmem, vmem, vmem),
        scratch_shapes=[
            pltpu.VMEM((27 * C, C), BF16),
            pltpu.VMEM((2, 3, 4, ROWS + 2, COLS, C), BF16),
            pltpu.VMEM((2, 2, 2, 3, 16, C), BF16),
            pltpu.VMEM((2, C, CELLS), BF16),
            pltpu.VMEM((2, 16, C), BF16),
            pltpu.VMEM((2, 16, C), F32),
            pltpu.VMEM((CELLS, 256), F32),
            pltpu.VMEM((8, 128), F32),
            pltpu.VMEM((HALF_TAPS * C + 96, 256), F32),
            pltpu.VMEM((4, 8 * WIN, 128), BF16),
            pltpu.VMEM((3, 8 * WIN, 128), BF16),
            pltpu.VMEM((2, 8, 128), F32),
            pltpu.VMEM((4, 8, 128), F32),
            pltpu.VMEM((8, WIN + 16, 128), BF16),
            pltpu.VMEM((8, WIN + 16, 128), BF16),
            pltpu.VMEM((192, 128), F32),
            pltpu.VMEM((8, 24, 128), F32),
            pltpu.VMEM((24, 128), F32),
            pltpu.VMEM((8, 24, 128), F32),
            pltpu.VMEM((96, 256), F32),
            dma(()),
            dma((17,)), dma((17,)), dma((3,)), dma((3,)),
            dma((PIECES, 3)), dma((PIECES, 3)), dma((4,)), dma((4,)),
            dma((8,)), dma((8,)), dma((8,)), dma((8,)), dma((8,)), dma((8,)),
        ],
        compiler_params=pltpu.CompilerParams(
            collective_id=0, has_side_effects=True, vmem_limit_bytes=48 * 1024 * 1024
        ),
    )(features, cotangent, kernel, gain.reshape(1, C))
    return fg, wg, gg[0, :C]


def solution(mesh):
    return jax.shard_map(
        per_device,
        mesh=mesh,
        in_specs=(P("tm", "row", "col", None), P("tm", "row", "col", None), P(), P()),
        out_specs=(P("tm", "row", "col", None), P(("row", "col"), None), P()),
        check_vma=False,
    )
```

time: 448 us -> 75.6 us (0.17)
  the two profiles are of different devices: /device:TPU:1 before, /device:TPU:22 now
where the time goes in v1:
time: 75.6 us; the launch traced here: 75.4 us
  Pallas kernels  69 us (91%)
  local copies, waits for them, and re-layouts  5.8 us (8%)
    pallas_call x1, Pallas kernels, per_device(): pl.pallas_call(body, out_shape=(jax.ShapeDtypeStruct((2, ROWS, COLS, C),...  69 us
    unnamed x10, local copies, waits for them, and re-layouts  5.8 us

profile of v1, /device:TPU:22, one launch (start us, length us, event | category | flops | bytes accessed | tf_op | source)
XLA Modules:
  0.0 75.4 jit_solution(4143140200663722218)
XLA Ops:
  0.6 0.0 copy-start.2
  0.6 0.0 copy-start.1
  0.7 0.0 copy-start
  0.7 3.9 %copy.7.w_hbm = bf16[5184,192]{1,0:T(8,128)(2,1)S(1)} copy(bf16[5184,192]{0,1:T(8,128)(2,1)} %param.6) | data formatting | bytes 3981312 | tf_op args[2]
  4.6 0.0 copy-done.2
  4.6 0.0 copy-done.1
  4.6 0.0 copy-done
  4.6 69.0 %shard_map.67 = (bf16[2,6,32,192]{3,2,1,0:T(8,128)(2,1)S(1)}, f32[81,192]{1,0:T(8,128)S(1)}, f32[1,256]{1,0:T(1,128)S(1)}) custom-call(bf16[2,6,32,192]{3,2,1,0:T(8,128)(2,1)S(1)} %copy-done, bf16[2,6,32,192]{3,2,1,0:T(8,128)(2,1)S(1)} %copy-done.1, bf16[5184,192]{1,0:T(8,128)(2,1)S(1)} %copy.7.w_hbm, f32[1,192]{1,0:T(1,128)S(1)} %bitcast.3), custom_call_target="tpu_custom_call" | custom-call | tf_op jit(solution)/shard_map/pallas_call | solution.py:356
  73.6 0.7 copy.11
  74.2 0.6 copy.12
  74.9 0.6 copy.13
Async XLA Ops:
  0.6 3.9 %copy-start.2 = (f32[192]{0:T(256)S(1)}, f32[192]{0:T(256)}, u32[]{:S(2)}) copy-start(f32[192]{0:T(256)} %param.7) | copy-start | bytes 2308
  0.6 3.9 %copy-start.1 = (bf16[2,6,32,192]{3,2,1,0:T(8,128)(2,1)S(1)}, bf16[2,6,32,192]{3,2,1,0:T(8,128)(2,1)}, u32[]{:S(2)}) copy-start(bf16[2,6,32,192]{3,2,1,0:T(8,128)(2,1)} %cot.1) | copy-start | bytes 442372
  0.7 3.9 %copy-start = (bf16[2,6,32,192]{3,2,1,0:T(8,128)(2,1)S(1)}, bf16[2,6,32,192]{3,2,1,0:T(8,128)(2,1)}, u32[]{:S(2)}) copy-start(bf16[2,6,32,192]{3,2,1,0:T(8,128)(2,1)} %feat.1) | copy-start | bytes 442372

commit v2 on v1

v2 whole, which is shorter than its diff:
```python
import math

import jax
import jax.numpy as jnp
from jax import lax
from jax.experimental import pallas as pl
from jax.experimental.pallas import tpu as pltpu
from jax.sharding import PartitionSpec as P

MESH = pl.DeviceIdType.MESH
F32 = jnp.float32
BF16 = jnp.bfloat16
C = 192
ROWS, COLS = 6, 32
CELLS = 2 * ROWS * COLS
HALF_TAPS = 14
SHARD = 81

HALO = [(1, 0, 0), (0, 1, 0), (1, 1, 0)]
HALO += [(df, out, dc) for df in (1, 0) for out in (0, 1) for dc in (-1, 1)]


def body(
    feat_hbm, cot_hbm, w_hbm, gain, fg_out, wg_out, gg_out,
    feat, cot, w_v, big, cols, act_t, packs, rows16, act32, wgl_a, wgl_b, xsend, xrecv,
    gpart, grecv_x, grecv_y, grecv_z, ysend, yrecv, zsend, zrecv, fin,
    in_sem, halo_s, halo_r, pair_s, pair_r, x_s, x_r, g_s, g_r, y_s, y_r, z_s, z_r, b_s, b_r,
):
    tm, row, col = lax.axis_index("tm"), lax.axis_index("row"), lax.axis_index("col")
    x, zlo = tm // 2, tm % 2
    y, core = row // 2, row % 2
    z = col * 2 + zlo
    other = 1 - core
    outward = 2 * core - 1
    partner = (tm, 2 * y + other, col)

    def near(dt, dr, dc):
        return ((tm + dt + 8) % 8, (row + dr + 16) % 16, (col + dc + 4) % 4)

    def x_dev(step):
        return (((x + step) % 4) * 2 + zlo, row, col)

    def y_dev(step):
        return (tm, (row + 2 * step) % 16, col)

    def z_dev(step):
        to = (z + step) % 8
        return (2 * x + to % 2, row, to // 2)

    def b_dev(step):
        return ((tm + step) % 8, row, col)

    def remote(src, dst, send, recv, device):
        return pltpu.make_async_remote_copy(
            src_ref=src, dst_ref=dst, send_sem=send, recv_sem=recv, device_id=device, device_id_type=MESH
        )

    main = big.at[0, 1]
    loads = [
        pltpu.make_async_copy(cot_hbm, cot, in_sem.at[0]),
        pltpu.make_async_copy(feat_hbm, feat, in_sem.at[1]),
        pltpu.make_async_copy(w_hbm, w_v, in_sem.at[2]),
    ]
    for copy in loads:
        copy.start()

    barrier = pltpu.get_barrier_semaphore()

    def greet(device):
        pl.semaphore_signal(barrier, inc=1, device_id=device, device_id_type=MESH)

    for df, out, dc in HALO:
        greet(near(df, outward * out, -dc))
    greet(partner)
    for step in range(1, 4):
        greet(x_dev(4 - step))
    for step in range(1, 8):
        greet(y_dev(8 - step))
        greet(z_dev(8 - step))
        greet(b_dev(8 - step))
    self_y = core == y // 4
    for k in range(8):
        @pl.when(jnp.logical_not(jnp.logical_and(self_y, y == k)))
        def _():
            greet((tm, 2 * k + y // 4, col))

    loads[0].wait()
    for side, q in ((0, 0), (1, COLS - 1)):
        rows16[side] = jnp.zeros((16, C), F32)
        for f in range(2):
            for r in range(ROWS):
                i = f * ROWS + r
                rows16[side, i : i + 1, :] = cot[f, r].astype(F32)[q : q + 1, :]
        packs[side] = rows16[side].astype(BF16)

    expected = len(HALO) + 1 + 3 + 7 + 7 + 7 + 8
    pl.semaphore_wait(barrier, expected - self_y.astype(jnp.int32))

    halo = []
    for m, (df, out, dc) in enumerate(HALO):
        if dc != 0:
            src = packs.at[0 if dc < 0 else 1]
            dst = cols.at[0, 1 if dc < 0 else 0, df, 2 * other if out else 1]
        elif out:
            src, dst = cot.at[:, (ROWS - 1) * core], main.at[2 * df : 2 * df + 2, (ROWS + 1) * other]
        else:
            src, dst = cot, main.at[2:4, 1 : ROWS + 1]
        halo.append(remote(src, dst, halo_s.at[m], halo_r.at[m], near(-df, outward * out, dc)))
        halo[-1].start()
    main[0:2, 1 : ROWS + 1] = cot[...]

    def norm():
        wide = feat[...].astype(F32).reshape(CELLS, C)
        inverse = lax.rsqrt(jnp.mean(wide * wide, axis=-1, keepdims=True) + 1e-06)
        normed = wide * inverse
        return inverse, normed, normed * gain[...]

    loads[1].wait()
    pre = norm()[2]
    act32[:, C:] = jnp.zeros((CELLS, 256 - C), F32)
    act32[:, :C] = pre * jax.nn.sigmoid(pre)
    act_t[0] = act32[...].T[:C].astype(BF16)
    swap = [remote(act_t.at[0], act_t.at[1], pair_s.at[0], pair_r.at[0], partner)]
    swap[0].start()

    for copy in halo:
        copy.wait_recv()

    @pl.when(row == 0)
    def _():
        main[:, 0] = jnp.zeros((4, COLS, C), BF16)
        cols[0, :, :, 0] = jnp.zeros((2, 2, 16, C), BF16)

    @pl.when(row == 15)
    def _():
        main[:, ROWS + 1] = jnp.zeros((4, COLS, C), BF16)
        cols[0, :, :, 2] = jnp.zeros((2, 2, 16, C), BF16)

    @pl.when(tm == 7)
    def _():
        main[2:4] = jnp.zeros((2, ROWS + 2, COLS, C), BF16)
        cols[0, :, 1] = jnp.zeros((2, 3, 16, C), BF16)

    @pl.when(col == 0)
    def _():
        cols[0, 0] = jnp.zeros((2, 3, 16, C), BF16)

    @pl.when(col == 3)
    def _():
        cols[0, 1] = jnp.zeros((2, 3, 16, C), BF16)

    swap.append(remote(main, big.at[1, 1], pair_s.at[1], pair_r.at[1], partner))
    swap.append(remote(cols.at[0], cols.at[1], pair_s.at[2], pair_r.at[2], partner))
    swap[1].start()
    swap[2].start()
    for copy in swap:
        copy.wait()
    main[:, (ROWS + 1) * other] = big[1, 1, :, 1 + (ROWS - 1) * core]
    big[1, 1, :, (ROWS + 1) * core] = main[:, ROWS - (ROWS - 1) * core]
    cols[0, :, :, 2 * other] = cols[1, :, :, 1]
    cols[1, :, :, 2 * core] = cols[0, :, :, 1]

    spot = lax.broadcasted_iota(jnp.int32, (COLS, C), 0)

    def shift(tile):
        for f in range(4):
            edges = [[cols[tile, s, f // 2, k].astype(F32) for k in range(3)] for s in (0, 1)]
            for r in range(ROWS + 2):
                k = 0 if r == 0 else 2 if r == ROWS + 1 else 1
                i = (f % 2) * ROWS + (r - 1) % ROWS
                value = big[tile, 1, f, r].astype(F32)
                after = jnp.where(spot == COLS - 1, edges[1][k][i : i + 1], pltpu.roll(value, COLS - 1, 0))
                before = jnp.where(spot == 0, edges[0][k][i : i + 1], pltpu.roll(value, 1, 0))
                big[tile, 0, f, r] = after.astype(BF16)
                big[tile, 2, f, r] = before.astype(BF16)

    shift(0)
    shift(1)

    for i in range(HALF_TAPS):
        tap = i + 13 * core
        a, b, c = tap // 9, (tap // 3) % 3, tap % 3
        total = jnp.zeros((C, C), F32)
        for tile in (0, 1):
            patch = big[tile, c, pl.ds(2 - a, 2), pl.ds(2 - b, ROWS)].reshape(CELLS, C)
            total += jnp.dot(act_t[tile], patch, preferred_element_type=F32)
        at = pl.multiple_of(i * C + 96 * other, 8)
        wgl_a[pl.ds(at, C), :] = total[:, 0:128]
        wgl_b[pl.ds(at, C), 0:64] = total[:, 128:C]

    lane = lax.broadcasted_iota(jnp.int32, (40, 128), 1)
    line = lax.broadcasted_iota(jnp.int32, (88, 128), 0)
    for j in range(32):
        at = 96 + SHARD * j
        upper = jnp.where(
            line < SHARD, wgl_a[at : at + 88], jnp.where(line == SHARD, wgl_b[at + 80 : at + 81], 0.0)
        )
        lower = jnp.where(lane < 64, wgl_b[at : at + 40], pltpu.roll(wgl_b[at + 40 : at + 80], 64, 1))
        value = jnp.concatenate([upper, lower], axis=0).astype(BF16)
        for k in range(4):
            xsend[k, j % 4, 32 * (j // 4) : 32 * (j // 4) + 32] = value[32 * k : 32 * k + 32]

    def x_copy(w, step):
        return remote(
            xsend.at[(x + step) % 4, w], xrecv.at[step - 1, w],
            x_s.at[w, step - 1], x_r.at[w, step - 1], x_dev(step),
        )

    def x_start(w):
        for step in (1, 2, 3):
            x_copy(w, step).start()

    x_start(0)
    x_start(1)

    loads[2].wait()
    dact = jnp.zeros((CELLS, C), F32)
    for tap in range(27):
        a, b, c = tap // 9, (tap // 3) % 3, tap % 3
        patch = big[0, c, 2 - a : 4 - a, 2 - b : 2 - b + ROWS].reshape(CELLS, C)
        dact += jnp.dot(patch, w_v[:, tap * C : (tap + 1) * C], preferred_element_type=F32)
    inverse, normed, pre = norm()
    sigma = jax.nn.sigmoid(pre)
    dpre = dact * sigma * (1.0 + pre * (1.0 - sigma))
    gain_part = jnp.sum(dpre * normed, axis=0, keepdims=True)
    dnormed = dpre * gain[...]
    project = jnp.mean(dnormed * normed, axis=-1, keepdims=True)
    grad = cot[...].astype(F32).reshape(CELLS, C) + inverse * (dnormed - normed * project)
    fg_out[...] = grad.astype(BF16).reshape(2, ROWS, COLS, C)

    act32[0:8, :] = jnp.zeros((8, 256), F32)
    act32[0:1, :C] = gain_part
    gpart[0] = act32[0:8, 0:128]
    gpart[0, 1:2] = act32[0:1, 128:256]
    gain_steps = [
        [remote(gpart.at[0], grecv_x.at[0], g_s.at[0], g_r.at[0], partner)],
        [remote(gpart.at[1], grecv_x.at[k], g_s.at[k], g_r.at[k], x_dev(k)) for k in range(1, 4)],
        [remote(gpart.at[2], grecv_y.at[k - 1], g_s.at[3 + k], g_r.at[3 + k], y_dev(k)) for k in range(1, 8)],
        [remote(gpart.at[3], grecv_z.at[k - 1], g_s.at[10 + k], g_r.at[10 + k], z_dev(k)) for k in range(1, 8)],
    ]

    def gain_begin(n):
        for copy in gain_steps[n]:
            copy.start()

    def gain_end(n):
        for copy in gain_steps[n]:
            copy.wait()
        total = gpart[n]
        arrived = [grecv_x[0:1], grecv_x[1:4], grecv_y[...], grecv_z[...]][n]
        for k in range(len(gain_steps[n])):
            total += arrived[k]
        gpart[n + 1] = total

    gain_begin(0)

    def y_copy(w, k):
        return remote(
            ysend.at[w, 32 * k : 32 * k + 32], yrecv.at[w, y], y_s.at[w, k], y_r.at[w, y],
            (tm, 8 * core + k, col),
        )

    def z_copy(w, k):
        return remote(
            zsend.at[w, 16 * k : 16 * k + 16], zrecv.at[z], z_s.at[w, k], z_r.at[z], (2 * x + k, row, w)
        )

    def over_y(w):
        for step in (1, 2, 3):
            x_copy(w, step).wait()
        if w + 2 < 4:
            x_start(w + 2)
        value = xsend[x, w].astype(F32)
        for step in (1, 2, 3):
            value += xrecv[step - 1, w].astype(F32)
        ysend[w] = value.astype(BF16)
        for k in range(8):
            mine = row == 8 * core + k

            @pl.when(jnp.logical_not(mine))
            def _():
                y_copy(w, k).start()

            @pl.when(mine)
            def _():
                yrecv[w, y] = ysend[w, 32 * k : 32 * k + 32]

    def over_z(w):
        for k in range(8):
            @pl.when(jnp.logical_not(jnp.logical_and(self_y, y == k)))
            def _():
                remote(ysend.at[w, 0:32], yrecv.at[w, k], y_s.at[w, 0], y_r.at[w, k], partner).wait_recv()

        total = yrecv[w, 0].astype(F32)
        for k in range(1, 8):
            total += yrecv[w, k].astype(F32)
        zsend[w] = total
        for k in range(2):
            @pl.when(z != 2 * w + k)
            def _():
                z_copy(w, k).start()

            @pl.when(z == 2 * w + k)
            def _():
                zrecv[z] = zsend[w, 16 * k : 16 * k + 16]

    over_y(0)
    gain_end(0)
    gain_begin(1)
    over_y(1)
    over_z(0)
    gain_end(1)
    gain_begin(2)
    over_y(2)
    over_z(1)
    gain_end(2)
    gain_begin(3)
    over_y(3)
    over_z(2)
    over_z(3)
    gain_end(3)

    for k in range(8):
        @pl.when(z != k)
        def _():
            remote(zsend.at[0, 0:16], zrecv.at[k], z_s.at[0, 0], z_r.at[k], partner).wait_recv()

    total = zrecv[0]
    for k in range(1, 8):
        total += zrecv[k]
    fin[tm] = total

    last = []
    for step in range(1, 8):
        last.append(remote(fin.at[tm], fin.at[tm], b_s.at[step - 1], b_r.at[step - 1], b_dev(step)))
        last[-1].start()
    for copy in last:
        copy.wait()

    scale = 1.0 / math.sqrt(16 * 96 * 128)
    gain_total = gpart[4] * scale
    gg_out[...] = jnp.concatenate([gain_total[0:1], gain_total[1:2]], axis=1)
    value = fin[...].reshape(128, 128) * scale
    wg_out[:, 0:128] = value[0:SHARD]
    wg_out[0:40, 128:C] = value[88:128, 0:64]
    wg_out[40:80, 128:C] = pltpu.roll(value[88:128], 64, 1)[:, 0:64]
    wg_out[80:81, 128:C] = value[81:82, 0:64]

    for copy in halo:
        copy.wait_send()
    for w in range(4):
        for k in range(8):
            @pl.when(row != 8 * core + k)
            def _():
                y_copy(w, k).wait_send()

        for k in range(2):
            @pl.when(z != 2 * w + k)
            def _():
                z_copy(w, k).wait_send()


def per_device(features, cotangent, kernel, gain):
    vmem = pl.BlockSpec(memory_space=pltpu.VMEM)
    hbm = pl.BlockSpec(memory_space=pltpu.HBM)
    dma = pltpu.SemaphoreType.DMA
    fg, wg, gg = pl.pallas_call(
        body,
        out_shape=(
            jax.ShapeDtypeStruct((2, ROWS, COLS, C), BF16),
            jax.ShapeDtypeStruct((SHARD, C), F32),
            jax.ShapeDtypeStruct((1, 256), F32),
        ),
        in_specs=[hbm, hbm, hbm, vmem],
        out_specs=(vmem, vmem, vmem),
        scratch_shapes=[
            pltpu.VMEM((2, ROWS, COLS, C), BF16),
            pltpu.VMEM((2, ROWS, COLS, C), BF16),
            pltpu.VMEM((C, 27 * C), BF16),
            pltpu.VMEM((2, 3, 4, ROWS + 2, COLS, C), BF16),
            pltpu.VMEM((2, 2, 2, 3, 16, C), BF16),
            pltpu.VMEM((2, C, CELLS), BF16),
            pltpu.VMEM((2, 16, C), BF16),
            pltpu.VMEM((2, 16, C), F32),
            pltpu.VMEM((CELLS, 256), F32),
            pltpu.VMEM((HALF_TAPS * C + 96, 128), F32),
            pltpu.VMEM((HALF_TAPS * C + 96, 128), F32),
            pltpu.VMEM((4, 4, 256, 128), BF16),
            pltpu.VMEM((3, 4, 256, 128), BF16),
            pltpu.VMEM((5, 8, 128), F32),
            pltpu.VMEM((4, 8, 128), F32),
            pltpu.VMEM((7, 8, 128), F32),
            pltpu.VMEM((7, 8, 128), F32),
            pltpu.VMEM((4, 256, 128), BF16),
            pltpu.VMEM((4, 8, 32, 128), BF16),
            pltpu.VMEM((4, 32, 128), F32),
            pltpu.VMEM((8, 16, 128), F32),
            pltpu.VMEM((8, 16, 128), F32),
            dma((3,)),
            dma((len(HALO),)), dma((len(HALO),)), dma((3,)), dma((3,)),
            dma((4, 3)), dma((4, 3)), dma((18,)), dma((18,)),
            dma((4, 8)), dma((4, 8)), dma((4, 2)), dma((8,)), dma((7,)), dma((7,)),
        ],
        compiler_params=pltpu.CompilerParams(
            collective_id=0, has_side_effects=True, vmem_limit_bytes=48 * 1024 * 1024
        ),
    )(features, cotangent, kernel.T, gain.reshape(1, C))
    return fg, wg, gg[0, :C]


def solution(mesh):
    return jax.shard_map(
        per_device,
        mesh=mesh,
        in_specs=(P("tm", "row", "col", None), P("tm", "row", "col", None), P(), P()),
        out_specs=(P("tm", "row", "col", None), P(("row", "col"), None), P()),
        check_vma=False,
    )
```

time: 75.6 us -> 64.7 us (0.86)
  the two profiles are of different devices: /device:TPU:22 before, /device:TPU:1 now
where the time goes in v2:
time: 64.7 us; the launch traced here: 64.4 us
  Pallas kernels  57.8 us (89%)
  local copies, waits for them, and re-layouts  5.97 us (9%)
  between operations  0.65 us (1%)
    pallas_call x1, Pallas kernels, per_device(): pl.pallas_call(body, out_shape=(jax.ShapeDtypeStruct((2, ROWS, COLS, C),...  57.8 us
    unnamed x11, local copies, waits for them, and re-layouts  5.97 us

profile of v2, /device:TPU:1, one launch (start us, length us, event | category | flops | bytes accessed | tf_op | source)
XLA Modules:
  0.0 64.4 jit_solution(6217080491400884865)
XLA Ops:
  0.6 0.0 copy-start
  0.6 1.6 %copy-done = bf16[5184,192]{0,1:T(8,128)(2,1)S(1)} copy-done((bf16[5184,192]{0,1:T(8,128)(2,1)S(1)}, bf16[5184,192]{0,1:T(8,128)(2,1)}, u32[]{:S(2)}) %copy-start) | copy-done | bytes 1990680
  2.2 0.0 copy-start.1
  2.2 0.9 %copy-done.1 = bf16[2,6,32,192]{3,2,1,0:T(8,128)(2,1)S(1)} copy-done((bf16[2,6,32,192]{3,2,1,0:T(8,128)(2,1)S(1)}, bf16[2,6,32,192]{3,2,1,0:T(8,128)(2,1)}, u32[]{:S(2)}) %copy-start.1) | copy-done | bytes 147480
  3.1 0.0 copy-start.2
  3.1 0.9 %copy-done.2 = bf16[2,6,32,192]{3,2,1,0:T(8,128)(2,1)S(1)} copy-done((bf16[2,6,32,192]{3,2,1,0:T(8,128)(2,1)S(1)}, bf16[2,6,32,192]{3,2,1,0:T(8,128)(2,1)}, u32[]{:S(2)}) %copy-start.2) | copy-done | bytes 147480
  4.0 0.0 copy-start.3
  4.1 0.7 %copy-done.3 = f32[192]{0:T(256)S(1)} copy-done((f32[192]{0:T(256)S(1)}, f32[192]{0:T(256)}, u32[]{:S(2)}) %copy-start.3) | copy-done | bytes 792
  4.7 57.8 %shard_map.67 = (bf16[2,6,32,192]{3,2,1,0:T(8,128)(2,1)S(1)}, f32[81,192]{1,0:T(8,128)S(1)}, f32[1,256]{1,0:T(1,128)S(1)}) custom-call(bf16[2,6,32,192]{3,2,1,0:T(8,128)(2,1)S(1)} %copy-done.1, bf16[2,6,32,192]{3,2,1,0:T(8,128)(2,1)S(1)} %copy-done.2, bf16[192,5184]{1,0:T(8,128)(2,1)S(1)} %bitcast.4, f32[1,192]{1,0:T(1,128)S(1)} %bitcast.5), custom_call_target="tpu_custom_call" | custom-call | tf_op jit(solution)/shard_map/pallas_call | solution.py:367
  62.6 0.7 %copy.10 = bf16[2,6,32,192]{3,2,1,0:T(8,128)(2,1)} copy(bf16[2,6,32,192]{3,2,1,0:T(8,128)(2,1)S(1)} %get-tuple-element.12) | data formatting | bytes 294912
  63.2 0.6 copy.11
  63.9 0.6 copy.12
Async XLA Ops:
  0.6 1.6 %copy-start = (bf16[5184,192]{0,1:T(8,128)(2,1)S(1)}, bf16[5184,192]{0,1:T(8,128)(2,1)}, u32[]{:S(2)}) copy-start(bf16[5184,192]{0,1:T(8,128)(2,1)} %param.6) | copy-start | bytes 5971972
  2.2 0.9 %copy-start.1 = (bf16[2,6,32,192]{3,2,1,0:T(8,128)(2,1)S(1)}, bf16[2,6,32,192]{3,2,1,0:T(8,128)(2,1)}, u32[]{:S(2)}) copy-start(bf16[2,6,32,192]{3,2,1,0:T(8,128)(2,1)} %feat_hbm.1) | copy-start | bytes 442372
  3.1 0.9 %copy-start.2 = (bf16[2,6,32,192]{3,2,1,0:T(8,128)(2,1)S(1)}, bf16[2,6,32,192]{3,2,1,0:T(8,128)(2,1)}, u32[]{:S(2)}) copy-start(bf16[2,6,32,192]{3,2,1,0:T(8,128)(2,1)} %cot_hbm.1) | copy-start | bytes 442372
  4.0 0.7 %copy-start.3 = (f32[192]{0:T(256)S(1)}, f32[192]{0:T(256)}, u32[]{:S(2)}) copy-start(f32[192]{0:T(256)} %param.7) | copy-start | bytes 2308

commit v3 on v2

--- a/solution.py
+++ b/solution.py
@@ -13,18 +13,19 @@
 C = 192
 ROWS, COLS = 6, 32
 CELLS = 2 * ROWS * COLS
-HALF_TAPS = 14
+LATE, EARLY = 11, 4
 SHARD = 81
 
-HALO = [(1, 0, 0), (0, 1, 0), (1, 1, 0)]
-HALO += [(df, out, dc) for df in (1, 0) for out in (0, 1) for dc in (-1, 1)]
+HALO = [(0, 1, 0)] + [(0, out, dc) for out in (0, 1) for dc in (-1, 1)]
+HALO += [(1, 0, 0), (1, 1, 0)] + [(1, out, dc) for out in (0, 1) for dc in (-1, 1)]
+NOW = 5
 
 
 def body(
     feat_hbm, cot_hbm, w_hbm, gain, fg_out, wg_out, gg_out,
-    feat, cot, w_v, big, cols, act_t, packs, rows16, act32, wgl_a, wgl_b, xsend, xrecv,
+    feat, cot, w_v, big, cols, act_t, packs, rows16, act32, wgl_a, wgl_b, xsend, xrecv, esend, erecv,
     gpart, grecv_x, grecv_y, grecv_z, ysend, yrecv, zsend, zrecv, fin,
-    in_sem, halo_s, halo_r, pair_s, pair_r, x_s, x_r, g_s, g_r, y_s, y_r, z_s, z_r, b_s, b_r,
+    in_sem, halo_s, halo_r, pair_s, pair_r, x_s, x_r, e_s, e_r, g_s, g_r, y_s, y_r, z_s, z_r, b_s, b_r,
 ):
     tm, row, col = lax.axis_index("tm"), lax.axis_index("row"), lax.axis_index("col")
     x, zlo = tm // 2, tm % 2
@@ -78,11 +79,12 @@
         greet(y_dev(8 - step))
         greet(z_dev(8 - step))
         greet(b_dev(8 - step))
-    self_y = core == y // 4
+    holder = jnp.logical_and(row >= 6, row < 14).astype(jnp.int32)
+    self_y = core == holder
     for k in range(8):
         @pl.when(jnp.logical_not(jnp.logical_and(self_y, y == k)))
         def _():
-            greet((tm, 2 * k + y // 4, col))
+            greet((tm, 2 * k + holder, col))
 
     loads[0].wait()
     for side, q in ((0, 0), (1, COLS - 1)):
@@ -100,7 +102,7 @@
     for m, (df, out, dc) in enumerate(HALO):
         if dc != 0:
             src = packs.at[0 if dc < 0 else 1]
-            dst = cols.at[0, 1 if dc < 0 else 0, df, 2 * other if out else 1]
+            dst = cols.at[0, df, 1 if dc < 0 else 0, 2 * other if out else 1]
         elif out:
             src, dst = cot.at[:, (ROWS - 1) * core], main.at[2 * df : 2 * df + 2, (ROWS + 1) * other]
         else:
@@ -123,48 +125,56 @@
     swap = [remote(act_t.at[0], act_t.at[1], pair_s.at[0], pair_r.at[0], partner)]
     swap[0].start()
 
-    for copy in halo:
-        copy.wait_recv()
-
-    @pl.when(row == 0)
-    def _():
-        main[:, 0] = jnp.zeros((4, COLS, C), BF16)
-        cols[0, :, :, 0] = jnp.zeros((2, 2, 16, C), BF16)
-
-    @pl.when(row == 15)
-    def _():
-        main[:, ROWS + 1] = jnp.zeros((4, COLS, C), BF16)
-        cols[0, :, :, 2] = jnp.zeros((2, 2, 16, C), BF16)
-
-    @pl.when(tm == 7)
-    def _():
-        main[2:4] = jnp.zeros((2, ROWS + 2, COLS, C), BF16)
-        cols[0, :, 1] = jnp.zeros((2, 3, 16, C), BF16)
-
-    @pl.when(col == 0)
-    def _():
-        cols[0, 0] = jnp.zeros((2, 3, 16, C), BF16)
-
-    @pl.when(col == 3)
-    def _():
-        cols[0, 1] = jnp.zeros((2, 3, 16, C), BF16)
-
-    swap.append(remote(main, big.at[1, 1], pair_s.at[1], pair_r.at[1], partner))
-    swap.append(remote(cols.at[0], cols.at[1], pair_s.at[2], pair_r.at[2], partner))
-    swap[1].start()
-    swap[2].start()
-    for copy in swap:
-        copy.wait()
-    main[:, (ROWS + 1) * other] = big[1, 1, :, 1 + (ROWS - 1) * core]
-    big[1, 1, :, (ROWS + 1) * core] = main[:, ROWS - (ROWS - 1) * core]
-    cols[0, :, :, 2 * other] = cols[1, :, :, 1]
-    cols[1, :, :, 2 * core] = cols[0, :, :, 1]
+    other_main = big.at[1, 1]
+
+    def borders(df):
+        f = slice(2 * df, 2 * df + 2)
+        for copy in halo[:NOW] if df == 0 else halo[NOW:]:
+            copy.wait_recv()
+
+        @pl.when(row == 0)
+        def _():
+            main[f, 0] = jnp.zeros((2, COLS, C), BF16)
+            cols[0, df, :, 0] = jnp.zeros((2, 16, C), BF16)
+
+        @pl.when(row == 15)
+        def _():
+            main[f, ROWS + 1] = jnp.zeros((2, COLS, C), BF16)
+            cols[0, df, :, 2] = jnp.zeros((2, 16, C), BF16)
+
+        if df == 1:
+            @pl.when(tm == 7)
+            def _():
+                main[f] = jnp.zeros((2, ROWS + 2, COLS, C), BF16)
+                cols[0, df] = jnp.zeros((2, 3, 16, C), BF16)
+
+        @pl.when(col == 0)
+        def _():
+            cols[0, df, 0] = jnp.zeros((3, 16, C), BF16)
+
+        @pl.when(col == 3)
+        def _():
+            cols[0, df, 1] = jnp.zeros((3, 16, C), BF16)
+
+        for copy in [
+            remote(main.at[f], other_main.at[f], pair_s.at[1 + 2 * df], pair_r.at[1 + 2 * df], partner),
+            remote(cols.at[0, df], cols.at[1, df], pair_s.at[2 + 2 * df], pair_r.at[2 + 2 * df], partner),
+        ]:
+            copy.start()
+            swap.append(copy)
+        for copy in swap:
+            copy.wait()
+        swap.clear()
+        main[f, (ROWS + 1) * other] = big[1, 1, f, 1 + (ROWS - 1) * core]
+        other_main[f, (ROWS + 1) * core] = main[f, ROWS - (ROWS - 1) * core]
+        cols[0, df, :, 2 * other] = cols[1, df, :, 1]
+        cols[1, df, :, 2 * core] = cols[0, df, :, 1]
 
     spot = lax.broadcasted_iota(jnp.int32, (COLS, C), 0)
 
-    def shift(tile):
-        for f in range(4):
-            edges = [[cols[tile, s, f // 2, k].astype(F32) for k in range(3)] for s in (0, 1)]
+    def shift(tile, df):
+        edges = [[cols[tile, df, s, k].astype(F32) for k in range(3)] for s in (0, 1)]
+        for f in (2 * df, 2 * df + 1):
             for r in range(ROWS + 2):
                 k = 0 if r == 0 else 2 if r == ROWS + 1 else 1
                 i = (f % 2) * ROWS + (r - 1) % ROWS
@@ -174,29 +184,52 @@
                 big[tile, 0, f, r] = after.astype(BF16)
                 big[tile, 2, f, r] = before.astype(BF16)
 
-    shift(0)
-    shift(1)
-
-    for i in range(HALF_TAPS):
-        tap = i + 13 * core
+    def tap_grad(tap, at):
         a, b, c = tap // 9, (tap // 3) % 3, tap % 3
         total = jnp.zeros((C, C), F32)
         for tile in (0, 1):
             patch = big[tile, c, pl.ds(2 - a, 2), pl.ds(2 - b, ROWS)].reshape(CELLS, C)
             total += jnp.dot(act_t[tile], patch, preferred_element_type=F32)
-        at = pl.multiple_of(i * C + 96 * other, 8)
+        at = pl.multiple_of(at, 8)
         wgl_a[pl.ds(at, C), :] = total[:, 0:128]
         wgl_b[pl.ds(at, C), 0:64] = total[:, 128:C]
 
     lane = lax.broadcasted_iota(jnp.int32, (40, 128), 1)
     line = lax.broadcasted_iota(jnp.int32, (88, 128), 0)
-    for j in range(32):
-        at = 96 + SHARD * j
+
+    def pack(at):
         upper = jnp.where(
             line < SHARD, wgl_a[at : at + 88], jnp.where(line == SHARD, wgl_b[at + 80 : at + 81], 0.0)
         )
         lower = jnp.where(lane < 64, wgl_b[at : at + 40], pltpu.roll(wgl_b[at + 40 : at + 80], 64, 1))
-        value = jnp.concatenate([upper, lower], axis=0).astype(BF16)
+        return jnp.concatenate([upper, lower], axis=0).astype(BF16)
+
+    def e_copy(step):
+        return remote(
+            esend.at[(x + step) % 4], erecv.at[step - 1], e_s.at[step - 1], e_r.at[step - 1], x_dev(step)
+        )
+
+    borders(0)
+    shift(0, 0)
+    shift(1, 0)
+    base = LATE * C + 24
+    for i in range(EARLY):
+        tap_grad(23 - 3 * core + i, base + i * C + 72 * core)
+    for j in range(8):
+        value = pack(base + 120 + SHARD * j)
+        at = 64 * (j % 4) + 32 * (j // 4)
+        for k in range(4):
+            esend[k, at : at + 32] = value[32 * k : 32 * k + 32]
+    for step in (1, 2, 3):
+        e_copy(step).start()
+
+    borders(1)
+    shift(0, 1)
+    shift(1, 1)
+    for i in range(LATE):
+        tap_grad(10 * core + i, i * C + 24 * other)
+    for j in range(24):
+        value = pack(24 + SHARD * j)
         for k in range(4):
             xsend[k, j % 4, 32 * (j // 4) : 32 * (j // 4) + 32] = value[32 * k : 32 * k + 32]
 
@@ -254,10 +287,13 @@
 
     gain_begin(0)
 
+    def y_row(k):
+        return k + 6 * core if k < 6 else k + 8 - 2 * core
+
     def y_copy(w, k):
         return remote(
             ysend.at[w, 32 * k : 32 * k + 32], yrecv.at[w, y], y_s.at[w, k], y_r.at[w, y],
-            (tm, 8 * core + k, col),
+            (tm, y_row(k), col),
         )
 
     def z_copy(w, k):
@@ -270,12 +306,16 @@
             x_copy(w, step).wait()
         if w + 2 < 4:
             x_start(w + 2)
+        part = slice(64 * w, 64 * w + 64)
         value = xsend[x, w].astype(F32)
+        extra = esend[x, part].astype(F32)
         for step in (1, 2, 3):
             value += xrecv[step - 1, w].astype(F32)
-        ysend[w] = value.astype(BF16)
+            extra += erecv[step - 1, part].astype(F32)
+        ysend[w, 0:192] = value.astype(BF16)
+        ysend[w, 192:256] = extra.astype(BF16)
         for k in range(8):
-            mine = row == 8 * core + k
+            mine = row == y_row(k)
 
             @pl.when(jnp.logical_not(mine))
             def _():
@@ -304,6 +344,8 @@
             def _():
                 zrecv[z] = zsend[w, 16 * k : 16 * k + 16]
 
+    for step in (1, 2, 3):
+        e_copy(step).wait()
     over_y(0)
     gain_end(0)
     gain_begin(1)
@@ -350,7 +392,7 @@
         copy.wait_send()
     for w in range(4):
         for k in range(8):
-            @pl.when(row != 8 * core + k)
+            @pl.when(row != y_row(k))
             def _():
                 y_copy(w, k).wait_send()
 
@@ -383,10 +425,12 @@
             pltpu.VMEM((2, 16, C), BF16),
             pltpu.VMEM((2, 16, C), F32),
             pltpu.VMEM((CELLS, 256), F32),
-            pltpu.VMEM((HALF_TAPS * C + 96, 128), F32),
-            pltpu.VMEM((HALF_TAPS * C + 96, 128), F32),
-            pltpu.VMEM((4, 4, 256, 128), BF16),
-            pltpu.VMEM((3, 4, 256, 128), BF16),
+            pltpu.VMEM(((LATE + EARLY) * C + 96, 128), F32),
+            pltpu.VMEM(((LATE + EARLY) * C + 96, 128), F32),
+            pltpu.VMEM((4, 4, 192, 128), BF16),
+            pltpu.VMEM((3, 4, 192, 128), BF16),
+            pltpu.VMEM((4, 256, 128), BF16),
+            pltpu.VMEM((3, 256, 128), BF16),
             pltpu.VMEM((5, 8, 128), F32),
             pltpu.VMEM((4, 8, 128), F32),
             pltpu.VMEM((7, 8, 128), F32),
@@ -397,12 +441,12 @@
             pltpu.VMEM((8, 16, 128), F32),
             pltpu.VMEM((8, 16, 128), F32),
             dma((3,)),
-            dma((len(HALO),)), dma((len(HALO),)), dma((3,)), dma((3,)),
-            dma((4, 3)), dma((4, 3)), dma((18,)), dma((18,)),
+            dma((len(HALO),)), dma((len(HALO),)), dma((5,)), dma((5,)),
+            dma((4, 3)), dma((4, 3)), dma((3,)), dma((3,)), dma((18,)), dma((18,)),
             dma((4, 8)), dma((4, 8)), dma((4, 2)), dma((8,)), dma((7,)), dma((7,)),
         ],
         compiler_params=pltpu.CompilerParams(
-            collective_id=0, has_side_effects=True, vmem_limit_bytes=48 * 1024 * 1024
+            collective_id=0, has_side_effects=True, vmem_limit_bytes=64 * 1024 * 1024 - 65536
         ),
     )(features, cotangent, kernel.T, gain.reshape(1, C))
     return fg, wg, gg[0, :C]

time: 64.7 us -> 61.9 us (0.957)
  local copies, waits for them, and re-layouts: 5.97 us -> 4.39 us
  Pallas kernels: 57.8 us -> 56.7 us
    unnamed x11 -> x3, local copies, waits for them, and re-layouts: 5.97 us -> 4.39 us
    pallas_call x1, Pallas kernels: 57.8 us -> 56.7 us  [per_device(): pl.pallas_call(body, out_shape=(jax.ShapeDtypeStruct((2, ROWS, COLS, C),...]
where the time goes in v3:
time: 61.9 us; the launch traced here: 61.7 us
  Pallas kernels  56.7 us (92%)
  local copies, waits for them, and re-layouts  4.39 us (7%)
  between operations  0.64 us (1%)
    pallas_call x1, Pallas kernels, per_device(): pl.pallas_call(body, out_shape=(jax.ShapeDtypeStruct((2, ROWS, COLS, C),...  56.7 us
    unnamed x3, local copies, waits for them, and re-layouts  4.39 us

profile of v3, /device:TPU:1, one launch (start us, length us, event | category | flops | bytes accessed | tf_op | source)
XLA Modules:
  0.0 61.7 jit_solution(2524232511095585111)
XLA Ops:
  0.6 56.7 %shard_map.67 = (bf16[2,6,32,192]{3,2,1,0:T(8,128)(2,1)}, f32[81,192]{1,0:T(8,128)}, f32[1,256]{1,0:T(1,128)}) custom-call(bf16[2,6,32,192]{3,2,1,0:T(8,128)(2,1)} %feat_hbm.1, bf16[2,6,32,192]{3,2,1,0:T(8,128)(2,1)} %cot_hbm.1, bf16[192,5184]{1,0:T(8,128)(2,1)} %bitcast.4, f32[1,192]{1,0:T(1,128)} %bitcast.5), custom_call_target="tpu_custom_call" | custom-call | tf_op jit(solution)/shard_map/pallas_call | solution.py:409
  57.3 1.6 %copy.10 = bf16[2,6,32,192]{3,2,1,0:T(8,128)(2,1)} copy(bf16[2,6,32,192]{3,2,1,0:T(8,128)(2,1)} %get-tuple-element.12) | data formatting | bytes 294912
  58.9 1.5 %copy.11 = f32[81,192]{1,0:T(8,128)} copy(f32[81,192]{1,0:T(8,128)} %get-tuple-element.13) | data formatting | bytes 124416
  60.5 1.2 %copy.12 = f32[192]{0:T(256)} copy(f32[192]{0:T(256)} %bitcast.6) | data formatting | bytes 1536

commit v4 on v3

--- a/solution.py
+++ b/solution.py
@@ -23,9 +23,9 @@
 
 def body(
     feat_hbm, cot_hbm, w_hbm, gain, fg_out, wg_out, gg_out,
-    feat, cot, w_v, big, cols, act_t, packs, rows16, act32, wgl_a, wgl_b, xsend, xrecv, esend, erecv,
+    feat, cot, w_v, big, cols, act_t, packs, rows16, act32, wgl_a, wgl_b, xsend, xrecv, esend, erecv, fsend, frecv, htotal, hsend, hrecv,
     gpart, grecv_x, grecv_y, grecv_z, ysend, yrecv, zsend, zrecv, fin,
-    in_sem, halo_s, halo_r, pair_s, pair_r, x_s, x_r, e_s, e_r, g_s, g_r, y_s, y_r, z_s, z_r, b_s, b_r,
+    in_sem, halo_s, halo_r, pair_s, pair_r, x_s, x_r, e_s, e_r, f_s, f_r, h_s, h_r, g_s, g_r, y_s, y_r, z_s, z_r, b_s, b_r,
 ):
     tm, row, col = lax.axis_index("tm"), lax.axis_index("row"), lax.axis_index("col")
     x, zlo = tm // 2, tm % 2
@@ -230,8 +230,50 @@
         tap_grad(10 * core + i, i * C + 24 * other)
     for j in range(24):
         value = pack(24 + SHARD * j)
-        for k in range(4):
-            xsend[k, j % 4, 32 * (j // 4) : 32 * (j // 4) + 32] = value[32 * k : 32 * k + 32]
+        if j % 4 == 3:
+            fsend[j // 4] = value
+        else:
+            for k in range(4):
+                xsend[k, j % 4, 32 * (j // 4) : 32 * (j // 4) + 32] = value[32 * k : 32 * k + 32]
+
+    def y_row(k):
+        return k + 6 * core if k < 6 else k + 8 - 2 * core
+
+    def f_copy(k):
+        return remote(fsend.at[k], frecv.at[y], f_s.at[k], f_r.at[y], (tm, y_row(k), col))
+
+    for k in range(6):
+        @pl.when(row != y_row(k))
+        def _():
+            f_copy(k).start()
+
+        @pl.when(row == y_row(k))
+        def _():
+            frecv[y] = fsend[k]
+
+    def h_copy(step):
+        return remote(
+            hsend.at[(x + step) % 4], hrecv.at[step - 1], h_s.at[step - 1], h_r.at[step - 1], x_dev(step)
+        )
+
+    def from_y(k):
+        return jnp.logical_not(jnp.logical_and(self_y, y == k))
+
+    def f_over_x():
+        @pl.when(row < 12)
+        def _():
+            for k in range(8):
+                @pl.when(from_y(k))
+                def _():
+                    remote(fsend.at[0], frecv.at[k], f_s.at[0], f_r.at[k], partner).wait_recv()
+
+            total = frecv[0].astype(F32)
+            for k in range(1, 8):
+                total += frecv[k].astype(F32)
+            htotal[...] = total.reshape(4, 32, 128)
+            hsend[...] = total.astype(BF16).reshape(4, 32, 128)
+            for step in (1, 2, 3):
+                h_copy(step).start()
 
     def x_copy(w, step):
         return remote(
@@ -287,9 +329,6 @@
 
     gain_begin(0)
 
-    def y_row(k):
-        return k + 6 * core if k < 6 else k + 8 - 2 * core
-
     def y_copy(w, k):
         return remote(
             ysend.at[w, 32 * k : 32 * k + 32], yrecv.at[w, y], y_s.at[w, k], y_r.at[w, y],
@@ -302,32 +341,32 @@
         )
 
     def over_y(w):
-        for step in (1, 2, 3):
-            x_copy(w, step).wait()
-        if w + 2 < 4:
-            x_start(w + 2)
         part = slice(64 * w, 64 * w + 64)
-        value = xsend[x, w].astype(F32)
         extra = esend[x, part].astype(F32)
         for step in (1, 2, 3):
-            value += xrecv[step - 1, w].astype(F32)
             extra += erecv[step - 1, part].astype(F32)
-        ysend[w, 0:192] = value.astype(BF16)
         ysend[w, 192:256] = extra.astype(BF16)
+        if w < 3:
+            for step in (1, 2, 3):
+                x_copy(w, step).wait()
+            if w == 0:
+                x_start(2)
+            value = xsend[x, w].astype(F32)
+            for step in (1, 2, 3):
+                value += xrecv[step - 1, w].astype(F32)
+            ysend[w, 0:192] = value.astype(BF16)
+        for k in range(8) if w < 3 else (6, 7):
+            @pl.when(row != y_row(k))
+            def _():
+                y_copy(w, k).start()
+
+            @pl.when(row == y_row(k))
+            def _():
+                yrecv[w, y] = ysend[w, 32 * k : 32 * k + 32]
+
+    def y_sum(w):
         for k in range(8):
-            mine = row == y_row(k)
-
-            @pl.when(jnp.logical_not(mine))
-            def _():
-                y_copy(w, k).start()
-
-            @pl.when(mine)
-            def _():
-                yrecv[w, y] = ysend[w, 32 * k : 32 * k + 32]
-
-    def over_z(w):
-        for k in range(8):
-            @pl.when(jnp.logical_not(jnp.logical_and(self_y, y == k)))
+            @pl.when(from_y(k))
             def _():
                 remote(ysend.at[w, 0:32], yrecv.at[w, k], y_s.at[w, 0], y_r.at[w, k], partner).wait_recv()
 
@@ -335,6 +374,24 @@
         for k in range(1, 8):
             total += yrecv[w, k].astype(F32)
         zsend[w] = total
+
+    def over_z(w):
+        if w < 3:
+            y_sum(w)
+        else:
+            @pl.when(row < 12)
+            def _():
+                for step in (1, 2, 3):
+                    h_copy(step).wait()
+                total = htotal[x]
+                for step in (1, 2, 3):
+                    total += hrecv[step - 1].astype(F32)
+                zsend[w] = total
+
+            @pl.when(row >= 12)
+            def _():
+                y_sum(w)
+
         for k in range(2):
             @pl.when(z != 2 * w + k)
             def _():
@@ -346,20 +403,21 @@
 
     for step in (1, 2, 3):
         e_copy(step).wait()
+    over_y(3)
     over_y(0)
     gain_end(0)
     gain_begin(1)
     over_y(1)
+    f_over_x()
     over_z(0)
     gain_end(1)
     gain_begin(2)
     over_y(2)
+    over_z(3)
     over_z(1)
     gain_end(2)
     gain_begin(3)
-    over_y(3)
     over_z(2)
-    over_z(3)
     gain_end(3)
 
     for k in range(8):
@@ -390,8 +448,13 @@
 
     for copy in halo:
         copy.wait_send()
+    for k in range(6):
+        @pl.when(row != y_row(k))
+        def _():
+            f_copy(k).wait_send()
+
     for w in range(4):
-        for k in range(8):
+        for k in range(8) if w < 3 else (6, 7):
             @pl.when(row != y_row(k))
             def _():
                 y_copy(w, k).wait_send()
@@ -427,10 +490,15 @@
             pltpu.VMEM((CELLS, 256), F32),
             pltpu.VMEM(((LATE + EARLY) * C + 96, 128), F32),
             pltpu.VMEM(((LATE + EARLY) * C + 96, 128), F32),
-            pltpu.VMEM((4, 4, 192, 128), BF16),
-            pltpu.VMEM((3, 4, 192, 128), BF16),
+            pltpu.VMEM((4, 3, 192, 128), BF16),
+            pltpu.VMEM((3, 3, 192, 128), BF16),
             pltpu.VMEM((4, 256, 128), BF16),
             pltpu.VMEM((3, 256, 128), BF16),
+            pltpu.VMEM((6, 128, 128), BF16),
+            pltpu.VMEM((8, 128, 128), BF16),
+            pltpu.VMEM((4, 32, 128), F32),
+            pltpu.VMEM((4, 32, 128), BF16),
+            pltpu.VMEM((3, 32, 128), BF16),
             pltpu.VMEM((5, 8, 128), F32),
             pltpu.VMEM((4, 8, 128), F32),
             pltpu.VMEM((7, 8, 128), F32),
@@ -442,11 +510,11 @@
             pltpu.VMEM((8, 16, 128), F32),
             dma((3,)),
             dma((len(HALO),)), dma((len(HALO),)), dma((5,)), dma((5,)),
-            dma((4, 3)), dma((4, 3)), dma((3,)), dma((3,)), dma((18,)), dma((18,)),
+            dma((3, 3)), dma((3, 3)), dma((3,)), dma((3,)), dma((6,)), dma((8,)), dma((3,)), dma((3,)), dma((18,)), dma((18,)),
             dma((4, 8)), dma((4, 8)), dma((4, 2)), dma((8,)), dma((7,)), dma((7,)),
         ],
         compiler_params=pltpu.CompilerParams(
-            collective_id=0, has_side_effects=True, vmem_limit_bytes=64 * 1024 * 1024 - 65536
+            collective_id=0, has_side_effects=True, vmem_limit_bytes=54912 * 1024
         ),
     )(features, cotangent, kernel.T, gain.reshape(1, C))
     return fg, wg, gg[0, :C]

time: 61.9 us -> 56.6 us (0.914)
  the two profiles are of different devices: /device:TPU:1 before, /device:TPU:8 now
where the time goes in v4:
time: 56.6 us; the launch traced here: 56.4 us
  Pallas kernels  53.2 us (94%)
  local copies, waits for them, and re-layouts  2.55 us (5%)
  between operations  0.65 us (1%)
    pallas_call x1, Pallas kernels, per_device(): pl.pallas_call(body, out_shape=(jax.ShapeDtypeStruct((2, ROWS, COLS, C),...  53.2 us
    unnamed x5, local copies, waits for them, and re-layouts  2.55 us

profile of v4, /device:TPU:8, one launch (start us, length us, event | category | flops | bytes accessed | tf_op | source)
XLA Modules:
  0.0 56.4 jit_solution(9479418665519817077)
XLA Ops:
  0.6 0.0 copy-start
  0.6 0.7 %copy-done = f32[192]{0:T(256)S(1)} copy-done((f32[192]{0:T(256)S(1)}, f32[192]{0:T(256)}, u32[]{:S(2)}) %copy-start) | copy-done | bytes 792
  1.3 53.2 %shard_map.67 = (bf16[2,6,32,192]{3,2,1,0:T(8,128)(2,1)S(1)}, f32[81,192]{1,0:T(8,128)S(1)}, f32[1,256]{1,0:T(1,128)S(1)}) custom-call(bf16[2,6,32,192]{3,2,1,0:T(8,128)(2,1)} %feat_hbm.1, bf16[2,6,32,192]{3,2,1,0:T(8,128)(2,1)} %cot_hbm.1, bf16[192,5184]{1,0:T(8,128)(2,1)} %bitcast.6, f32[1,192]{1,0:T(1,128)S(1)} %bitcast.4), custom_call_target="tpu_custom_call" | custom-call | tf_op jit(solution)/shard_map/pallas_call | solution.py:472
  54.5 0.7 %copy.10 = bf16[2,6,32,192]{3,2,1,0:T(8,128)(2,1)} copy(bf16[2,6,32,192]{3,2,1,0:T(8,128)(2,1)S(1)} %get-tuple-element.12) | data formatting | bytes 294912
  55.2 0.6 %copy.11 = f32[81,192]{1,0:T(8,128)} copy(f32[81,192]{1,0:T(8,128)S(1)} %get-tuple-element.13) | data formatting | bytes 124416
  55.9 0.6 copy.12
Async XLA Ops:
  0.6 0.7 %copy-start = (f32[192]{0:T(256)S(1)}, f32[192]{0:T(256)}, u32[]{:S(2)}) copy-start(f32[192]{0:T(256)} %param.7) | copy-start | bytes 2308

commit v5 on v4

--- a/solution.py
+++ b/solution.py
@@ -24,7 +24,7 @@
 def body(
     feat_hbm, cot_hbm, w_hbm, gain, fg_out, wg_out, gg_out,
     feat, cot, w_v, big, cols, act_t, packs, rows16, act32, wgl_a, wgl_b, xsend, xrecv, esend, erecv, fsend, frecv, htotal, hsend, hrecv,
-    gpart, grecv_x, grecv_y, grecv_z, ysend, yrecv, zsend, zrecv, fin,
+    gpart, grecv, ysend, yrecv, zsend, zrecv, fin,
     in_sem, halo_s, halo_r, pair_s, pair_r, x_s, x_r, e_s, e_r, f_s, f_r, h_s, h_r, g_s, g_r, y_s, y_r, z_s, z_r, b_s, b_r,
 ):
     tm, row, col = lax.axis_index("tm"), lax.axis_index("row"), lax.axis_index("col")
@@ -41,9 +41,6 @@
     def x_dev(step):
         return (((x + step) % 4) * 2 + zlo, row, col)
 
-    def y_dev(step):
-        return (tm, (row + 2 * step) % 16, col)
-
     def z_dev(step):
         to = (z + step) % 8
         return (2 * x + to % 2, row, to // 2)
@@ -76,7 +73,6 @@
     for step in range(1, 4):
         greet(x_dev(4 - step))
     for step in range(1, 8):
-        greet(y_dev(8 - step))
         greet(z_dev(8 - step))
         greet(b_dev(8 - step))
     holder = jnp.logical_and(row >= 6, row < 14).astype(jnp.int32)
@@ -95,7 +91,7 @@
                 rows16[side, i : i + 1, :] = cot[f, r].astype(F32)[q : q + 1, :]
         packs[side] = rows16[side].astype(BF16)
 
-    expected = len(HALO) + 1 + 3 + 7 + 7 + 7 + 8
+    expected = len(HALO) + 1 + 3 + 7 + 7 + 8
     pl.semaphore_wait(barrier, expected - self_y.astype(jnp.int32))
 
     halo = []
@@ -307,31 +303,18 @@
     act32[0:1, :C] = gain_part
     gpart[0] = act32[0:8, 0:128]
     gpart[0, 1:2] = act32[0:1, 128:256]
-    gain_steps = [
-        [remote(gpart.at[0], grecv_x.at[0], g_s.at[0], g_r.at[0], partner)],
-        [remote(gpart.at[1], grecv_x.at[k], g_s.at[k], g_r.at[k], x_dev(k)) for k in range(1, 4)],
-        [remote(gpart.at[2], grecv_y.at[k - 1], g_s.at[3 + k], g_r.at[3 + k], y_dev(k)) for k in range(1, 8)],
-        [remote(gpart.at[3], grecv_z.at[k - 1], g_s.at[10 + k], g_r.at[10 + k], z_dev(k)) for k in range(1, 8)],
+    gain_pair = remote(gpart.at[0], grecv.at[0], g_s.at[0], g_r.at[0], partner)
+    gain_pair.start()
+    gain_cols = [
+        remote(gpart.at[1], grecv.at[k], g_s.at[k], g_r.at[k], (tm, row, (col + k) % 4)) for k in (1, 2, 3)
     ]
 
-    def gain_begin(n):
-        for copy in gain_steps[n]:
-            copy.start()
-
-    def gain_end(n):
-        for copy in gain_steps[n]:
-            copy.wait()
-        total = gpart[n]
-        arrived = [grecv_x[0:1], grecv_x[1:4], grecv_y[...], grecv_z[...]][n]
-        for k in range(len(gain_steps[n])):
-            total += arrived[k]
-        gpart[n + 1] = total
-
-    gain_begin(0)
+    def y_part(w):
+        return slice(0, 48 if w == 0 else 32)
 
     def y_copy(w, k):
         return remote(
-            ysend.at[w, 32 * k : 32 * k + 32], yrecv.at[w, y], y_s.at[w, k], y_r.at[w, y],
+            ysend.at[w, k, y_part(w)], yrecv.at[w, y, y_part(w)], y_s.at[w, k], y_r.at[w, y],
             (tm, y_row(k), col),
         )
 
@@ -345,7 +328,7 @@
         extra = esend[x, part].astype(F32)
         for step in (1, 2, 3):
             extra += erecv[step - 1, part].astype(F32)
-        ysend[w, 192:256] = extra.astype(BF16)
+        ysend[w, 6:8, 0:32] = extra.astype(BF16).reshape(2, 32, 128)
         if w < 3:
             for step in (1, 2, 3):
                 x_copy(w, step).wait()
@@ -354,7 +337,14 @@
             value = xsend[x, w].astype(F32)
             for step in (1, 2, 3):
                 value += xrecv[step - 1, w].astype(F32)
-            ysend[w, 0:192] = value.astype(BF16)
+            ysend[w, 0:6, 0:32] = value.astype(BF16).reshape(6, 32, 128)
+        if w == 0:
+            gain_pair.wait()
+            total = gpart[0] + grecv[0]
+            upper = total.astype(BF16).astype(F32)
+            both = jnp.concatenate([upper, total - upper], axis=0).astype(BF16)
+            for k in range(8):
+                ysend[w, k, 32:48] = both
         for k in range(8) if w < 3 else (6, 7):
             @pl.when(row != y_row(k))
             def _():
@@ -362,18 +352,22 @@
 
             @pl.when(row == y_row(k))
             def _():
-                yrecv[w, y] = ysend[w, 32 * k : 32 * k + 32]
+                yrecv[w, y, y_part(w)] = ysend[w, k, y_part(w)]
 
     def y_sum(w):
         for k in range(8):
             @pl.when(from_y(k))
             def _():
-                remote(ysend.at[w, 0:32], yrecv.at[w, k], y_s.at[w, 0], y_r.at[w, k], partner).wait_recv()
-
-        total = yrecv[w, 0].astype(F32)
+                remote(
+                    ysend.at[w, 0, y_part(w)], yrecv.at[w, k, y_part(w)], y_s.at[w, 0], y_r.at[w, k], partner
+                ).wait_recv()
+
+        total = yrecv[w, 0, y_part(w)].astype(F32)
         for k in range(1, 8):
-            total += yrecv[w, k].astype(F32)
-        zsend[w] = total
+            total += yrecv[w, k, y_part(w)].astype(F32)
+        zsend[w] = total[0:32]
+        if w == 0:
+            gpart[1] = total[32:40] + total[40:48]
 
     def over_z(w):
         if w < 3:
@@ -405,20 +399,15 @@
         e_copy(step).wait()
     over_y(3)
     over_y(0)
-    gain_end(0)
-    gain_begin(1)
     over_y(1)
     f_over_x()
+    over_y(2)
     over_z(0)
-    gain_end(1)
-    gain_begin(2)
-    over_y(2)
+    for copy in gain_cols:
+        copy.start()
     over_z(3)
     over_z(1)
-    gain_end(2)
-    gain_begin(3)
     over_z(2)
-    gain_end(3)
 
     for k in range(8):
         @pl.when(z != k)
@@ -428,41 +417,47 @@
     total = zrecv[0]
     for k in range(1, 8):
         total += zrecv[k]
-    fin[tm] = total
+    fin[tm, 0:16] = total
+    for copy in gain_cols:
+        copy.wait()
+    fin[tm, 16:24] = gpart[1] + grecv[1] + grecv[2] + grecv[3]
 
     last = []
     for step in range(1, 8):
         last.append(remote(fin.at[tm], fin.at[tm], b_s.at[step - 1], b_r.at[step - 1], b_dev(step)))
         last[-1].start()
+
+    for copy in halo:
+        copy.wait_send()
+    for k in range(6):
+        @pl.when(row != y_row(k))
+        def _():
+            f_copy(k).wait_send()
+
+    for w in range(4):
+        for k in range(8) if w < 3 else (6, 7):
+            @pl.when(row != y_row(k))
+            def _():
+                y_copy(w, k).wait_send()
+
+        for k in range(2):
+            @pl.when(z != 2 * w + k)
+            def _():
+                z_copy(w, k).wait_send()
+
     for copy in last:
         copy.wait()
-
     scale = 1.0 / math.sqrt(16 * 96 * 128)
-    gain_total = gpart[4] * scale
+    gain_total = fin[0, 16:24]
+    for k in range(1, 8):
+        gain_total += fin[k, 16:24]
+    gain_total *= scale
     gg_out[...] = jnp.concatenate([gain_total[0:1], gain_total[1:2]], axis=1)
-    value = fin[...].reshape(128, 128) * scale
+    value = fin[:, 0:16].reshape(128, 128) * scale
     wg_out[:, 0:128] = value[0:SHARD]
     wg_out[0:40, 128:C] = value[88:128, 0:64]
     wg_out[40:80, 128:C] = pltpu.roll(value[88:128], 64, 1)[:, 0:64]
     wg_out[80:81, 128:C] = value[81:82, 0:64]
-
-    for copy in halo:
-        copy.wait_send()
-    for k in range(6):
-        @pl.when(row != y_row(k))
-        def _():
-            f_copy(k).wait_send()
-
-    for w in range(4):
-        for k in range(8) if w < 3 else (6, 7):
-            @pl.when(row != y_row(k))
-            def _():
-                y_copy(w, k).wait_send()
-
-        for k in range(2):
-            @pl.when(z != 2 * w + k)
-            def _():
-                z_copy(w, k).wait_send()
 
 
 def per_device(features, cotangent, kernel, gain):
@@ -499,18 +494,16 @@
             pltpu.VMEM((4, 32, 128), F32),
             pltpu.VMEM((4, 32, 128), BF16),
             pltpu.VMEM((3, 32, 128), BF16),
-            pltpu.VMEM((5, 8, 128), F32),
+            pltpu.VMEM((2, 8, 128), F32),
             pltpu.VMEM((4, 8, 128), F32),
-            pltpu.VMEM((7, 8, 128), F32),
-            pltpu.VMEM((7, 8, 128), F32),
-            pltpu.VMEM((4, 256, 128), BF16),
-            pltpu.VMEM((4, 8, 32, 128), BF16),
+            pltpu.VMEM((4, 8, 48, 128), BF16),
+            pltpu.VMEM((4, 8, 48, 128), BF16),
             pltpu.VMEM((4, 32, 128), F32),
             pltpu.VMEM((8, 16, 128), F32),
-            pltpu.VMEM((8, 16, 128), F32),
+            pltpu.VMEM((8, 24, 128), F32),
             dma((3,)),
             dma((len(HALO),)), dma((len(HALO),)), dma((5,)), dma((5,)),
-            dma((3, 3)), dma((3, 3)), dma((3,)), dma((3,)), dma((6,)), dma((8,)), dma((3,)), dma((3,)), dma((18,)), dma((18,)),
+            dma((3, 3)), dma((3, 3)), dma((3,)), dma((3,)), dma((6,)), dma((8,)), dma((3,)), dma((3,)), dma((4,)), dma((4,)),
             dma((4, 8)), dma((4, 8)), dma((4, 2)), dma((8,)), dma((7,)), dma((7,)),
         ],
         compiler_params=pltpu.CompilerParams(

time: 56.6 us -> 52.8 us (0.933)
  the two profiles are of different devices: /device:TPU:8 before, /device:TPU:1 now
where the time goes in v5:
time: 52.8 us; the launch traced here: 52.7 us
  Pallas kernels  49.5 us (94%)
  local copies, waits for them, and re-layouts  2.55 us (5%)
  between operations  0.65 us (1%)
    pallas_call x1, Pallas kernels, per_device(): pl.pallas_call(body, out_shape=(jax.ShapeDtypeStruct((2, ROWS, COLS, C),...  49.5 us
    unnamed x5, local copies, waits for them, and re-layouts  2.55 us

profile of v5, /device:TPU:1, one launch (start us, length us, event | category | flops | bytes accessed | tf_op | source)
XLA Modules:
  0.0 52.7 jit_solution(7419196692190082098)
XLA Ops:
  0.6 0.0 copy-start
  0.6 0.7 %copy-done = f32[192]{0:T(256)S(1)} copy-done((f32[192]{0:T(256)S(1)}, f32[192]{0:T(256)}, u32[]{:S(2)}) %copy-start) | copy-done | bytes 792
  1.3 49.5 %shard_map.67 = (bf16[2,6,32,192]{3,2,1,0:T(8,128)(2,1)S(1)}, f32[81,192]{1,0:T(8,128)S(1)}, f32[1,256]{1,0:T(1,128)S(1)}) custom-call(bf16[2,6,32,192]{3,2,1,0:T(8,128)(2,1)} %feat_hbm.1, bf16[2,6,32,192]{3,2,1,0:T(8,128)(2,1)} %cot_hbm.1, bf16[192,5184]{1,0:T(8,128)(2,1)} %bitcast.6, f32[1,192]{1,0:T(1,128)S(1)} %bitcast.4), custom_call_target="tpu_custom_call" | custom-call | tf_op jit(solution)/shard_map/pallas_call | solution.py:467
  50.8 0.7 %copy.10 = bf16[2,6,32,192]{3,2,1,0:T(8,128)(2,1)} copy(bf16[2,6,32,192]{3,2,1,0:T(8,128)(2,1)S(1)} %get-tuple-element.12) | data formatting | bytes 294912
  51.5 0.6 %copy.11 = f32[81,192]{1,0:T(8,128)} copy(f32[81,192]{1,0:T(8,128)S(1)} %get-tuple-element.13) | data formatting | bytes 124416
  52.1 0.6 %copy.12 = f32[192]{0:T(256)} copy(f32[192]{0:T(256)S(1)} %bitcast.5) | data formatting | bytes 1536
Async XLA Ops:
  0.6 0.7 %copy-start = (f32[192]{0:T(256)S(1)}, f32[192]{0:T(256)}, u32[]{:S(2)}) copy-start(f32[192]{0:T(256)} %param.7) | copy-start | bytes 2308

commit v6 on v5

--- a/solution.py
+++ b/solution.py
@@ -25,7 +25,7 @@
     feat_hbm, cot_hbm, w_hbm, gain, fg_out, wg_out, gg_out,
     feat, cot, w_v, big, cols, act_t, packs, rows16, act32, wgl_a, wgl_b, xsend, xrecv, esend, erecv, fsend, frecv, htotal, hsend, hrecv,
     gpart, grecv, ysend, yrecv, zsend, zrecv, fin,
-    in_sem, halo_s, halo_r, pair_s, pair_r, x_s, x_r, e_s, e_r, f_s, f_r, h_s, h_r, g_s, g_r, y_s, y_r, z_s, z_r, b_s, b_r,
+    in_sem, halo_s, halo_r, tile_s, tile_r, pair_s, pair_r, x_s, x_r, e_s, e_r, f_s, f_r, h_s, h_r, g_s, g_r, y_s, y_r, z_s, z_r, b_s, b_r,
 ):
     tm, row, col = lax.axis_index("tm"), lax.axis_index("row"), lax.axis_index("col")
     x, zlo = tm // 2, tm % 2
@@ -94,7 +94,7 @@
     expected = len(HALO) + 1 + 3 + 7 + 7 + 8
     pl.semaphore_wait(barrier, expected - self_y.astype(jnp.int32))
 
-    halo = []
+    halo, tile = [], []
     for m, (df, out, dc) in enumerate(HALO):
         if dc != 0:
             src = packs.at[0 if dc < 0 else 1]
@@ -102,9 +102,23 @@
         elif out:
             src, dst = cot.at[:, (ROWS - 1) * core], main.at[2 * df : 2 * df + 2, (ROWS + 1) * other]
         else:
-            src, dst = cot, main.at[2:4, 1 : ROWS + 1]
+            for f in (0, 1):
+                tile.append(remote(
+                    cot.at[f], main.at[2 + f, 1 : ROWS + 1], tile_s.at[f], tile_r.at[f], near(-1, 0, 0)
+                ))
+                tile[-1].start()
+            continue
         halo.append(remote(src, dst, halo_s.at[m], halo_r.at[m], near(-df, outward * out, dc)))
         halo[-1].start()
+
+    other_main = big.at[1, 1]
+    swap = []
+
+    def hand_over(n, src, dst):
+        swap.append(remote(src, dst, pair_s.at[n], pair_r.at[n], partner))
+        swap[-1].start()
+
+    hand_over(0, cot, other_main.at[0:2, 1 : ROWS + 1])
     main[0:2, 1 : ROWS + 1] = cot[...]
 
     def norm():
@@ -118,13 +132,20 @@
     act32[:, C:] = jnp.zeros((CELLS, 256 - C), F32)
     act32[:, :C] = pre * jax.nn.sigmoid(pre)
     act_t[0] = act32[...].T[:C].astype(BF16)
-    swap = [remote(act_t.at[0], act_t.at[1], pair_s.at[0], pair_r.at[0], partner)]
-    swap[0].start()
-
-    other_main = big.at[1, 1]
+    hand_over(1, act_t.at[0], act_t.at[1])
 
     def borders(df):
         f = slice(2 * df, 2 * df + 2)
+        if df == 1:
+            for n in (0, 1):
+                tile[n].wait_recv()
+
+                @pl.when(tm == 7)
+                def _():
+                    main[2 + n, 1 : ROWS + 1] = jnp.zeros((ROWS, COLS, C), BF16)
+
+                inner = (2 + n, slice(1, ROWS + 1))
+                hand_over(4 + n, main.at[inner], other_main.at[inner])
         for copy in halo[:NOW] if df == 0 else halo[NOW:]:
             copy.wait_recv()
 
@@ -141,7 +162,7 @@
         if df == 1:
             @pl.when(tm == 7)
             def _():
-                main[f] = jnp.zeros((2, ROWS + 2, COLS, C), BF16)
+                main[f, (ROWS + 1) * core] = jnp.zeros((2, COLS, C), BF16)
                 cols[0, df] = jnp.zeros((2, 3, 16, C), BF16)
 
         @pl.when(col == 0)
@@ -152,12 +173,9 @@
         def _():
             cols[0, df, 1] = jnp.zeros((3, 16, C), BF16)
 
-        for copy in [
-            remote(main.at[f], other_main.at[f], pair_s.at[1 + 2 * df], pair_r.at[1 + 2 * df], partner),
-            remote(cols.at[0, df], cols.at[1, df], pair_s.at[2 + 2 * df], pair_r.at[2 + 2 * df], partner),
-        ]:
-            copy.start()
-            swap.append(copy)
+        edge = (ROWS + 1) * core
+        hand_over(2 + 4 * df, main.at[f, edge], other_main.at[f, edge])
+        hand_over(3 + 4 * df, cols.at[0, df], cols.at[1, df])
         for copy in swap:
             copy.wait()
         swap.clear()
@@ -205,6 +223,22 @@
             esend.at[(x + step) % 4], erecv.at[step - 1], e_s.at[step - 1], e_r.at[step - 1], x_dev(step)
         )
 
+    def y_row(k):
+        return k + 6 * core if k < 6 else k + 8 - 2 * core
+
+    def f_copy(k):
+        return remote(fsend.at[k], frecv.at[y], f_s.at[k], f_r.at[y], (tm, y_row(k), col))
+
+    def f_start(chunks):
+        for k in chunks:
+            @pl.when(row != y_row(k))
+            def _():
+                f_copy(k).start()
+
+            @pl.when(row == y_row(k))
+            def _():
+                frecv[y] = fsend[k]
+
     borders(0)
     shift(0, 0)
     shift(1, 0)
@@ -214,10 +248,14 @@
     for j in range(8):
         value = pack(base + 120 + SHARD * j)
         at = 64 * (j % 4) + 32 * (j // 4)
-        for k in range(4):
-            esend[k, at : at + 32] = value[32 * k : 32 * k + 32]
+        if j % 4 == 3:
+            fsend[6 + j // 4] = value
+        else:
+            for k in range(4):
+                esend[k, at : at + 32] = value[32 * k : 32 * k + 32]
     for step in (1, 2, 3):
         e_copy(step).start()
+    f_start((6, 7))
 
     borders(1)
     shift(0, 1)
@@ -232,20 +270,7 @@
             for k in range(4):
                 xsend[k, j % 4, 32 * (j // 4) : 32 * (j // 4) + 32] = value[32 * k : 32 * k + 32]
 
-    def y_row(k):
-        return k + 6 * core if k < 6 else k + 8 - 2 * core
-
-    def f_copy(k):
-        return remote(fsend.at[k], frecv.at[y], f_s.at[k], f_r.at[y], (tm, y_row(k), col))
-
-    for k in range(6):
-        @pl.when(row != y_row(k))
-        def _():
-            f_copy(k).start()
-
-        @pl.when(row == y_row(k))
-        def _():
-            frecv[y] = fsend[k]
+    f_start(range(6))
 
     def h_copy(step):
         return remote(
@@ -256,20 +281,18 @@
         return jnp.logical_not(jnp.logical_and(self_y, y == k))
 
     def f_over_x():
-        @pl.when(row < 12)
-        def _():
-            for k in range(8):
-                @pl.when(from_y(k))
-                def _():
-                    remote(fsend.at[0], frecv.at[k], f_s.at[0], f_r.at[k], partner).wait_recv()
-
-            total = frecv[0].astype(F32)
-            for k in range(1, 8):
-                total += frecv[k].astype(F32)
-            htotal[...] = total.reshape(4, 32, 128)
-            hsend[...] = total.astype(BF16).reshape(4, 32, 128)
-            for step in (1, 2, 3):
-                h_copy(step).start()
+        for k in range(8):
+            @pl.when(from_y(k))
+            def _():
+                remote(fsend.at[0], frecv.at[k], f_s.at[0], f_r.at[k], partner).wait_recv()
+
+        total = frecv[0].astype(F32)
+        for k in range(1, 8):
+            total += frecv[k].astype(F32)
+        htotal[...] = total.reshape(4, 32, 128)
+        hsend[...] = total.astype(BF16).reshape(4, 32, 128)
+        for step in (1, 2, 3):
+            h_copy(step).start()
 
     def x_copy(w, step):
         return remote(
@@ -329,15 +352,14 @@
         for step in (1, 2, 3):
             extra += erecv[step - 1, part].astype(F32)
         ysend[w, 6:8, 0:32] = extra.astype(BF16).reshape(2, 32, 128)
-        if w < 3:
-            for step in (1, 2, 3):
-                x_copy(w, step).wait()
-            if w == 0:
-                x_start(2)
-            value = xsend[x, w].astype(F32)
-            for step in (1, 2, 3):
-                value += xrecv[step - 1, w].astype(F32)
-            ysend[w, 0:6, 0:32] = value.astype(BF16).reshape(6, 32, 128)
+        for step in (1, 2, 3):
+            x_copy(w, step).wait()
+        if w == 0:
+            x_start(2)
+        value = xsend[x, w].astype(F32)
+        for step in (1, 2, 3):
+            value += xrecv[step - 1, w].astype(F32)
+        ysend[w, 0:6, 0:32] = value.astype(BF16).reshape(6, 32, 128)
         if w == 0:
             gain_pair.wait()
             total = gpart[0] + grecv[0]
@@ -345,7 +367,7 @@
             both = jnp.concatenate([upper, total - upper], axis=0).astype(BF16)
             for k in range(8):
                 ysend[w, k, 32:48] = both
-        for k in range(8) if w < 3 else (6, 7):
+        for k in range(8):
             @pl.when(row != y_row(k))
             def _():
                 y_copy(w, k).start()
@@ -373,18 +395,12 @@
         if w < 3:
             y_sum(w)
         else:
-            @pl.when(row < 12)
-            def _():
-                for step in (1, 2, 3):
-                    h_copy(step).wait()
-                total = htotal[x]
-                for step in (1, 2, 3):
-                    total += hrecv[step - 1].astype(F32)
-                zsend[w] = total
-
-            @pl.when(row >= 12)
-            def _():
-                y_sum(w)
+            for step in (1, 2, 3):
+                h_copy(step).wait()
+            total = htotal[x]
+            for step in (1, 2, 3):
+                total += hrecv[step - 1].astype(F32)
+            zsend[w] = total
 
         for k in range(2):
             @pl.when(z != 2 * w + k)
@@ -397,7 +413,6 @@
 
     for step in (1, 2, 3):
         e_copy(step).wait()
-    over_y(3)
     over_y(0)
     over_y(1)
     f_over_x()
@@ -427,19 +442,16 @@
         last.append(remote(fin.at[tm], fin.at[tm], b_s.at[step - 1], b_r.at[step - 1], b_dev(step)))
         last[-1].start()
 
-    for copy in halo:
+    for copy in halo + tile:
         copy.wait_send()
-    for k in range(6):
+    for k in range(8):
         @pl.when(row != y_row(k))
         def _():
             f_copy(k).wait_send()
+            for w in range(3):
+                y_copy(w, k).wait_send()
 
     for w in range(4):
-        for k in range(8) if w < 3 else (6, 7):
-            @pl.when(row != y_row(k))
-            def _():
-                y_copy(w, k).wait_send()
-
         for k in range(2):
             @pl.when(z != 2 * w + k)
             def _():
@@ -487,24 +499,24 @@
             pltpu.VMEM(((LATE + EARLY) * C + 96, 128), F32),
             pltpu.VMEM((4, 3, 192, 128), BF16),
             pltpu.VMEM((3, 3, 192, 128), BF16),
-            pltpu.VMEM((4, 256, 128), BF16),
-            pltpu.VMEM((3, 256, 128), BF16),
-            pltpu.VMEM((6, 128, 128), BF16),
+            pltpu.VMEM((4, 192, 128), BF16),
+            pltpu.VMEM((3, 192, 128), BF16),
+            pltpu.VMEM((8, 128, 128), BF16),
             pltpu.VMEM((8, 128, 128), BF16),
             pltpu.VMEM((4, 32, 128), F32),
             pltpu.VMEM((4, 32, 128), BF16),
             pltpu.VMEM((3, 32, 128), BF16),
             pltpu.VMEM((2, 8, 128), F32),
             pltpu.VMEM((4, 8, 128), F32),
-            pltpu.VMEM((4, 8, 48, 128), BF16),
-            pltpu.VMEM((4, 8, 48, 128), BF16),
+            pltpu.VMEM((3, 8, 48, 128), BF16),
+            pltpu.VMEM((3, 8, 48, 128), BF16),
             pltpu.VMEM((4, 32, 128), F32),
             pltpu.VMEM((8, 16, 128), F32),
             pltpu.VMEM((8, 24, 128), F32),
             dma((3,)),
-            dma((len(HALO),)), dma((len(HALO),)), dma((5,)), dma((5,)),
-            dma((3, 3)), dma((3, 3)), dma((3,)), dma((3,)), dma((6,)), dma((8,)), dma((3,)), dma((3,)), dma((4,)), dma((4,)),
-            dma((4, 8)), dma((4, 8)), dma((4, 2)), dma((8,)), dma((7,)), dma((7,)),
+            dma((len(HALO),)), dma((len(HALO),)), dma((2,)), dma((2,)), dma((8,)), dma((8,)),
+            dma((3, 3)), dma((3, 3)), dma((3,)), dma((3,)), dma((8,)), dma((8,)), dma((3,)), dma((3,)), dma((4,)), dma((4,)),
+            dma((3, 8)), dma((3, 8)), dma((4, 2)), dma((8,)), dma((7,)), dma((7,)),
         ],
         compiler_params=pltpu.CompilerParams(
             collective_id=0, has_side_effects=True, vmem_limit_bytes=54912 * 1024

time: 52.8 us -> 52.1 us (0.987); the launches traced: 52.7 us -> 51.4 us
  Pallas kernels: 49.5 us -> 48.2 us
    pallas_call x1, Pallas kernels: 49.5 us -> 48.2 us  [per_device(): pl.pallas_call(body, out_shape=(jax.ShapeDtypeStruct((2, ROWS, COLS, C),...]
where the time goes in v6:
time: 52.1 us; the launch traced here: 51.4 us
  Pallas kernels  48.2 us (93%)
  local copies, waits for them, and re-layouts  2.55 us (5%)
  between operations  0.65 us (1%)
    pallas_call x1, Pallas kernels, per_device(): pl.pallas_call(body, out_shape=(jax.ShapeDtypeStruct((2, ROWS, COLS, C),...  48.2 us
    unnamed x5, local copies, waits for them, and re-layouts  2.55 us

profile of v6, /device:TPU:1, one launch (start us, length us, event | category | flops | bytes accessed | tf_op | source)
XLA Modules:
  0.0 51.4 jit_solution(2021950682742231045)
XLA Ops:
  0.6 0.0 copy-start
  0.6 0.7 %copy-done = f32[192]{0:T(256)S(1)} copy-done((f32[192]{0:T(256)S(1)}, f32[192]{0:T(256)}, u32[]{:S(2)}) %copy-start) | copy-done | bytes 792
  1.3 48.2 %shard_map.67 = (bf16[2,6,32,192]{3,2,1,0:T(8,128)(2,1)S(1)}, f32[81,192]{1,0:T(8,128)S(1)}, f32[1,256]{1,0:T(1,128)S(1)}) custom-call(bf16[2,6,32,192]{3,2,1,0:T(8,128)(2,1)} %feat_hbm.1, bf16[2,6,32,192]{3,2,1,0:T(8,128)(2,1)} %cot_hbm.1, bf16[192,5184]{1,0:T(8,128)(2,1)} %bitcast.6, f32[1,192]{1,0:T(1,128)S(1)} %bitcast.4), custom_call_target="tpu_custom_call" | custom-call | tf_op jit(solution)/shard_map/pallas_call | solution.py:479
  49.6 0.7 %copy.10 = bf16[2,6,32,192]{3,2,1,0:T(8,128)(2,1)} copy(bf16[2,6,32,192]{3,2,1,0:T(8,128)(2,1)S(1)} %get-tuple-element.12) | data formatting | bytes 294912
  50.2 0.6 %copy.11 = f32[81,192]{1,0:T(8,128)} copy(f32[81,192]{1,0:T(8,128)S(1)} %get-tuple-element.13) | data formatting | bytes 124416
  50.9 0.6 %copy.12 = f32[192]{0:T(256)} copy(f32[192]{0:T(256)S(1)} %bitcast.5) | data formatting | bytes 1536
Async XLA Ops:
  0.6 0.7 %copy-start = (f32[192]{0:T(256)S(1)}, f32[192]{0:T(256)}, u32[]{:S(2)}) copy-start(f32[192]{0:T(256)} %param.7) | copy-start | bytes 2308

commit v7 on v6

--- a/solution.py
+++ b/solution.py
@@ -23,7 +23,7 @@
 
 def body(
     feat_hbm, cot_hbm, w_hbm, gain, fg_out, wg_out, gg_out,
-    feat, cot, w_v, big, cols, act_t, packs, rows16, act32, wgl_a, wgl_b, xsend, xrecv, esend, erecv, fsend, frecv, htotal, hsend, hrecv,
+    feat, cot, tsend, trecv, w_v, big, cols, act_t, packs, rows16, act32, wgl_a, wgl_b, xsend, xrecv, esend, erecv, fsend, frecv, htotal, hsend, hrecv,
     gpart, grecv, ysend, yrecv, zsend, zrecv, fin,
     in_sem, halo_s, halo_r, tile_s, tile_r, pair_s, pair_r, x_s, x_r, e_s, e_r, f_s, f_r, h_s, h_r, g_s, g_r, y_s, y_r, z_s, z_r, b_s, b_r,
 ):
@@ -91,6 +91,14 @@
                 rows16[side, i : i + 1, :] = cot[f, r].astype(F32)[q : q + 1, :]
         packs[side] = rows16[side].astype(BF16)
 
+    half = CELLS // 2
+    act32[:, :C] = cot[...].astype(F32).reshape(CELLS, C)
+    side = lax.broadcasted_iota(jnp.int32, (half, 128), 1)
+    rest = jnp.where(side < 64, act32[0:half, 128:256], pltpu.roll(act32[half:CELLS, 128:256], 64, 1))
+    tsend[0] = cot[0, :, :, 0:128]
+    tsend[1] = rest.astype(BF16).reshape(ROWS, COLS, 128)
+    tsend[2] = cot[1, :, :, 0:128]
+
     expected = len(HALO) + 1 + 3 + 7 + 7 + 8
     pl.semaphore_wait(barrier, expected - self_y.astype(jnp.int32))
 
@@ -102,9 +110,9 @@
         elif out:
             src, dst = cot.at[:, (ROWS - 1) * core], main.at[2 * df : 2 * df + 2, (ROWS + 1) * other]
         else:
-            for f in (0, 1):
+            for n, part in enumerate((slice(0, 2), slice(2, 3))):
                 tile.append(remote(
-                    cot.at[f], main.at[2 + f, 1 : ROWS + 1], tile_s.at[f], tile_r.at[f], near(-1, 0, 0)
+                    tsend.at[part], trecv.at[part], tile_s.at[n], tile_r.at[n], near(-1, 0, 0)
                 ))
                 tile[-1].start()
             continue
@@ -139,6 +147,10 @@
         if df == 1:
             for n in (0, 1):
                 tile[n].wait_recv()
+                rest = trecv[1].astype(F32).reshape(CELLS // 2, 128)
+                rest = rest if n == 0 else pltpu.roll(rest, 64, 1)
+                main[2 + n, 1 : ROWS + 1, :, 0:128] = trecv[2 * n]
+                main[2 + n, 1 : ROWS + 1, :, 128:C] = rest[:, 0:64].astype(BF16).reshape(ROWS, COLS, 64)
 
                 @pl.when(tm == 7)
                 def _():
@@ -488,6 +500,8 @@
         scratch_shapes=[
             pltpu.VMEM((2, ROWS, COLS, C), BF16),
             pltpu.VMEM((2, ROWS, COLS, C), BF16),
+            pltpu.VMEM((3, ROWS, COLS, 128), BF16),
+            pltpu.VMEM((3, ROWS, COLS, 128), BF16),
             pltpu.VMEM((C, 27 * C), BF16),
             pltpu.VMEM((2, 3, 4, ROWS + 2, COLS, C), BF16),
             pltpu.VMEM((2, 2, 2, 3, 16, C), BF16),

time: 52.1 us -> 51.3 us (0.985); the launches traced: 51.4 us -> 51.2 us
  no operation moved by 1% of the time
where the time goes in v7:
time: 51.3 us; the launch traced here: 51.2 us
  Pallas kernels  48 us (94%)
  local copies, waits for them, and re-layouts  2.55 us (5%)
  between operations  0.65 us (1%)
    pallas_call x1, Pallas kernels, per_device(): pl.pallas_call(body, out_shape=(jax.ShapeDtypeStruct((2, ROWS, COLS, C),...  48 us
    unnamed x5, local copies, waits for them, and re-layouts  2.55 us

profile of v7, /device:TPU:1, one launch (start us, length us, event | category | flops | bytes accessed | tf_op | source)
XLA Modules:
  0.0 51.2 jit_solution(14128332480415617650)
XLA Ops:
  0.6 0.0 copy-start
  0.6 0.7 %copy-done = f32[192]{0:T(256)S(1)} copy-done((f32[192]{0:T(256)S(1)}, f32[192]{0:T(256)}, u32[]{:S(2)}) %copy-start) | copy-done | bytes 792
  1.3 48.0 %shard_map.67 = (bf16[2,6,32,192]{3,2,1,0:T(8,128)(2,1)S(1)}, f32[81,192]{1,0:T(8,128)S(1)}, f32[1,256]{1,0:T(1,128)S(1)}) custom-call(bf16[2,6,32,192]{3,2,1,0:T(8,128)(2,1)} %feat_hbm.1, bf16[2,6,32,192]{3,2,1,0:T(8,128)(2,1)} %cot_hbm.1, bf16[192,5184]{1,0:T(8,128)(2,1)} %bitcast.6, f32[1,192]{1,0:T(1,128)S(1)} %bitcast.4), custom_call_target="tpu_custom_call" | custom-call | tf_op jit(solution)/shard_map/pallas_call | solution.py:491
  49.3 0.7 %copy.10 = bf16[2,6,32,192]{3,2,1,0:T(8,128)(2,1)} copy(bf16[2,6,32,192]{3,2,1,0:T(8,128)(2,1)S(1)} %get-tuple-element.12) | data formatting | bytes 294912
  50.0 0.6 %copy.11 = f32[81,192]{1,0:T(8,128)} copy(f32[81,192]{1,0:T(8,128)S(1)} %get-tuple-element.13) | data formatting | bytes 124416
  50.6 0.6 %copy.12 = f32[192]{0:T(256)} copy(f32[192]{0:T(256)S(1)} %bitcast.5) | data formatting | bytes 1536
Async XLA Ops:
  0.6 0.7 %copy-start = (f32[192]{0:T(256)S(1)}, f32[192]{0:T(256)}, u32[]{:S(2)}) copy-start(f32[192]{0:T(256)} %param.7) | copy-start | bytes 2308

commit v8 on v7

--- a/solution.py
+++ b/solution.py
@@ -17,7 +17,7 @@
 SHARD = 81
 
 HALO = [(0, 1, 0)] + [(0, out, dc) for out in (0, 1) for dc in (-1, 1)]
-HALO += [(1, 0, 0), (1, 1, 0)] + [(1, out, dc) for out in (0, 1) for dc in (-1, 1)]
+HALO += [(1, out, dc) for out in (0, 1) for dc in (-1, 1)] + [(1, 1, 0), (1, 0, 0)]
 NOW = 5
 
 

time: 51.3 us -> 50.1 us (0.977)
  Pallas kernels: 48 us -> 46.8 us
    pallas_call x1, Pallas kernels: 48 us -> 46.8 us  [per_device(): pl.pallas_call(body, out_shape=(jax.ShapeDtypeStruct((2, ROWS, COLS, C),...]
where the time goes in v8:
time: 50.1 us; the launch traced here: 50 us
  Pallas kernels  46.8 us (93%)
  local copies, waits for them, and re-layouts  2.55 us (5%)
  between operations  0.65 us (1%)
    pallas_call x1, Pallas kernels, per_device(): pl.pallas_call(body, out_shape=(jax.ShapeDtypeStruct((2, ROWS, COLS, C),...  46.8 us
    unnamed x5, local copies, waits for them, and re-layouts  2.55 us

profile of v8, /device:TPU:1, one launch (start us, length us, event | category | flops | bytes accessed | tf_op | source)
XLA Modules:
  0.0 50.0 jit_solution(11134095067476664520)
XLA Ops:
  0.6 0.0 copy-start
  0.6 0.7 %copy-done = f32[192]{0:T(256)S(1)} copy-done((f32[192]{0:T(256)S(1)}, f32[192]{0:T(256)}, u32[]{:S(2)}) %copy-start) | copy-done | bytes 792
  1.3 46.8 %shard_map.67 = (bf16[2,6,32,192]{3,2,1,0:T(8,128)(2,1)S(1)}, f32[81,192]{1,0:T(8,128)S(1)}, f32[1,256]{1,0:T(1,128)S(1)}) custom-call(bf16[2,6,32,192]{3,2,1,0:T(8,128)(2,1)} %feat_hbm.1, bf16[2,6,32,192]{3,2,1,0:T(8,128)(2,1)} %cot_hbm.1, bf16[192,5184]{1,0:T(8,128)(2,1)} %bitcast.6, f32[1,192]{1,0:T(1,128)S(1)} %bitcast.4), custom_call_target="tpu_custom_call" | custom-call | tf_op jit(solution)/shard_map/pallas_call | solution.py:491
  48.1 0.7 %copy.10 = bf16[2,6,32,192]{3,2,1,0:T(8,128)(2,1)} copy(bf16[2,6,32,192]{3,2,1,0:T(8,128)(2,1)S(1)} %get-tuple-element.12) | data formatting | bytes 294912
  48.8 0.6 %copy.11 = f32[81,192]{1,0:T(8,128)} copy(f32[81,192]{1,0:T(8,128)S(1)} %get-tuple-element.13) | data formatting | bytes 124416
  49.4 0.6 %copy.12 = f32[192]{0:T(256)} copy(f32[192]{0:T(256)S(1)} %bitcast.5) | data formatting | bytes 1536
Async XLA Ops:
  0.6 0.7 %copy-start = (f32[192]{0:T(256)S(1)}, f32[192]{0:T(256)}, u32[]{:S(2)}) copy-start(f32[192]{0:T(256)} %param.7) | copy-start | bytes 2308
